TPU v7x, 512 devices: a whole 4x8x8 slice. The times are simulated.
512 devices in a mesh: row: 4 (over y_hi), col: 16 (over x, y_lo, core), layer: 8 (over z).
Axes of the slice: x: 4, y: 8 (y_hi: 4, y_lo: 2; y = y_hi * 2 + y_lo), z: 8, core: 2. Of those that a mesh axis runs over, the one named last changes fastest.
Arguments:
- density: float32 [4096, 4096], P(('row', 'layer'), 'col'), as said below
- pattern: int32 [32, 32], replicated, may hold values from 0 to 1, as said below
Outputs:
- square: float32 [4096, 4096], P(('row', 'layer'), 'col')
- purified: float32 [4096, 4096], P(('row', 'layer'), 'col')
Inputs may be any that keep to these rules, and one draw needn't show every extreme that they name: pattern is symmetric, holds only 0 and 1, and its diagonal is 1. density is symmetric.
All inputs are finite; a program needn't handle non-finite values.
Results may differ from a plain program's by a relative error of at most 0.0001.
Values sent between devices are 32-bit elements; how exact they have to be, the bound alone decides.
No kernel may reach another device: no remote copies, remote signals or barrier semaphores. Data moves between devices by JAX's collectives and lax.ppermute only.
A program may use at most 64 MiB of HBM per device.

v0:
```python
import jax
import jax.numpy as jnp
from jax import lax
from jax.sharding import PartitionSpec as P

BLK = 128


def layer_order(full_rows, row_count, layer_count):
    slab_rows, order = full_rows.shape
    shard = order // (row_count * layer_count)
    split = full_rows.reshape(slab_rows, row_count, layer_count, shard)
    return split.transpose(2, 0, 1, 3).reshape(layer_count, slab_rows, row_count * shard)


def body(density, pattern):
    layer_count = lax.axis_size("layer")
    row_count = lax.axis_size("row")
    slab_rows, slab_width = density.shape
    row_start = (lax.axis_index("row") * layer_count + lax.axis_index("layer")) * slab_rows
    row_blocks = (row_start + jnp.arange(slab_rows, dtype=jnp.int32)) // BLK
    col_blocks = (
        lax.axis_index("col") * slab_width + jnp.arange(slab_width, dtype=jnp.int32)
    ) // BLK
    local_mask = jnp.take(jnp.take(pattern, row_blocks, axis=0), col_blocks, axis=1)
    masked = density * local_mask.astype(jnp.float32)
    full_rows = lax.all_gather(masked, "col", axis=1, tiled=True)
    left_panel = lax.all_to_all(
        layer_order(full_rows, row_count, layer_count),
        "layer",
        split_axis=0,
        concat_axis=1,
        tiled=True,
    )[0]
    right_panel = lax.all_gather(masked, "row", axis=0, tiled=True)
    square_terms = jnp.dot(
        left_panel, right_panel, precision=lax.Precision.HIGHEST, preferred_element_type=jnp.float32
    )
    square = lax.psum_scatter(square_terms, "layer", scatter_dimension=0, tiled=True)
    square_rows = lax.all_gather(square, "col", axis=1, tiled=True)
    square_left = lax.all_to_all(
        layer_order(square_rows, row_count, layer_count),
        "layer",
        split_axis=0,
        concat_axis=1,
        tiled=True,
    )[0]
    cube_terms = jnp.dot(
        square_left,
        right_panel,
        precision=lax.Precision.HIGHEST,
        preferred_element_type=jnp.float32,
    )
    cube = lax.psum_scatter(cube_terms, "layer", scatter_dimension=0, tiled=True)
    return (square, 3.0 * square - 2.0 * cube)


def solution(mesh):
    in_specs = (P(("row", "layer"), "col"), P())
    out_specs = (P(("row", "layer"), "col"), P(("row", "layer"), "col"))
    return jax.shard_map(body, mesh=mesh, in_specs=in_specs, out_specs=out_specs, check_vma=False)
```

profile of v0, /device:TPU:1, one launch (start us, length us, event | category | flops | bytes accessed | tf_op | source)
XLA Modules:
  0.0 308.1 jit_solution(2794929155609538790)
XLA Ops:
  7.3 0.5 copy-done
  7.9 0.6 gather_fusion
  8.5 0.1 broadcast_select_fusion
  8.6 0.1 copy.10
  8.7 1.0 copy.11
  9.7 0.7 gather_fusion.1
  10.4 0.8 bitcast_multiply_fusion
  11.2 45.4 %all-gather.3.cloned.1.call-done = f32[128,4096]{0,1:T(8,128)} async-done(((f32[128,256]{0,1:T(8,128)}), f32[128,4096]{0,1:T(8,128)}) %all-gather.3.cloned.1.call-update) | async-done | bytes 2097168 | tf_op jit(solution)/shard_map/all_gather | solution.py:27
  56.6 3.1 %copy.12 = f32[128,4,8,128]{0,3,1,2:T(8,128)} copy(f32[128,4,8,128]{0,3,2,1:T(8,128)} %bitcast.26) | data formatting | bytes 4194304 | tf_op jit(solution)/shard_map/reshape | solution.py:12
  59.7 7.2 %all-to-all-start = ((f32[8,128,512]{1,2,0:T(8,128)}), f32[8,128,512]{1,2,0:T(8,128)}, u32[]{:S(2)}, u32[]{:S(2)}) async-start(f32[8,128,512]{1,2,0:T(8,128)} %bitcast.5), calls=%async_computation | async-start | bytes 4194304 | tf_op jit(solution)/shard_map/all_to_all | solution.py:28
  67.0 15.6 %all_gather.10 = f32[512,256]{0,1:T(8,128)S(1)} all-gather(f32[128,256]{0,1:T(8,128)S(1)} %copy-done.1), channel_id=1, replica_groups=mesh['row'=4,'col'=16,'layer'=8] {'row'}, dimensions={0}, use_global_device_ids=true | all-gather | bytes 655360 | tf_op jit(solution)/shard_map/all_gather | solution.py:35
  82.6 32.8 %all-to-all-done = f32[8,128,512]{1,2,0:T(8,128)} async-done(((f32[8,128,512]{1,2,0:T(8,128)}), f32[8,128,512]{1,2,0:T(8,128)}, u32[]{:S(2)}, u32[]{:S(2)}) %all-to-all-start) | async-done | bytes 2097184 | tf_op jit(solution)/shard_map/all_to_all | solution.py:28
  115.4 1.9 copy.13
  117.3 2.8 fusion.1
  120.1 0.0 all-gather.5.cloned.1.call-start
  120.2 35.2 %reduce-scatter.3.cloned.1.call-done = f32[128,256]{1,0:T(8,128)} async-done(((f32[1024,256]{1,0:T(8,128)}), f32[128,256]{1,0:T(8,128)}) %reduce-scatter.3.cloned.1.call-update) | async-done | bytes 131088 | tf_op jit(solution)/shard_map/reduce_scatter | solution.py:39
  155.5 45.1 %all-gather.5.cloned.1.call-done = f32[128,4096]{1,0:T(8,128)} async-done(((f32[128,256]{1,0:T(8,128)}), f32[128,4096]{1,0:T(8,128)}) %all-gather.5.cloned.1.call-update) | async-done | bytes 2097168 | tf_op jit(solution)/shard_map/all_gather | solution.py:40
  200.6 2.0 copy.16
  202.5 1.9 copy.14
  204.4 58.3 %all_to_all.8 = f32[8,128,512]{1,2,0:T(8,128)} all-to-all(f32[8,128,512]{1,2,0:T(8,128)} %bitcast.24), channel_id=1, replica_groups=mesh['row'=4,'col'=16,'layer'=8] {'layer'}, dimensions={0} | all-to-all | bytes 4194304 | tf_op jit(solution)/shard_map/all_to_all | solution.py:41
  262.7 1.9 copy.15
  264.7 2.8 fusion.2
  267.5 32.5 %reduce-scatter.5.cloned.1.call-done = f32[128,256]{1,0:T(8,128)} async-done(((f32[1024,256]{1,0:T(8,128)}), f32[128,256]{1,0:T(8,128)}) %reduce-scatter.5.cloned.1.call-update) | async-done | bytes 131088 | tf_op jit(solution)/shard_map/reduce_scatter | solution.py:54
  300.0 1.6 multiply_subtract_fusion
  (18 shorter events, 0.3 us)
Async XLA Ops:
  7.2 0.7 copy-start
  7.2 49.4 %all-gather.3.cloned.1.call-start = ((), (), s32[]{:S(2)}) async-start(), calls=%async_computation.4 | async-start | bytes 2228224 | tf_op jit(solution)/shard_map/all_gather | solution.py:27
  59.7 7.3 %copy-start.1 = (f32[128,256]{0,1:T(8,128)S(1)}, f32[128,256]{0,1:T(8,128)}, u32[]{:S(2)}) copy-start(f32[128,256]{0,1:T(8,128)} %bitcast_multiply_fusion) | copy-start | bytes 393220
  59.7 55.6 %all-to-all-start = ((f32[8,128,512]{1,2,0:T(8,128)}), f32[8,128,512]{1,2,0:T(8,128)}, u32[]{:S(2)}, u32[]{:S(2)}) async-start(f32[8,128,512]{1,2,0:T(8,128)} %bitcast.5), calls=%async_computation | async-start | bytes 4194304 | tf_op jit(solution)/shard_map/all_to_all | solution.py:28
  67.0 88.5 %reduce-scatter.3.cloned.1.call-start = ((), (), s32[]{:S(2)}) async-start(), calls=%async_computation.5 | async-start | bytes 1179648 | tf_op jit(solution)/shard_map/reduce_scatter | solution.py:39
  120.1 80.4 %all-gather.5.cloned.1.call-start = ((), (), s32[]{:S(2)}) async-start(), calls=%async_computation.6 | async-start | bytes 2228224 | tf_op jit(solution)/shard_map/all_gather | solution.py:40
  155.5 144.5 %reduce-scatter.5.cloned.1.call-start = ((), (), s32[]{:S(2)}) async-start(), calls=%async_computation.7 | async-start | bytes 1179648 | tf_op jit(solution)/shard_map/reduce_scatter | solution.py:54
  264.6 35.3 %copy-start.2 = (f32[128,256]{1,0:T(8,128)S(1)}, f32[128,256]{1,0:T(8,128)}, u32[]{:S(2)}) copy-start(f32[128,256]{1,0:T(8,128)} %reduce-scatter.3.cloned.1.call-done) | copy-start | bytes 393220
Sparse Core Ops, SparseCore 0:
  11.3 45.2 all-gather.2
  120.3 35.1 reduce-scatter.2
  158.1 42.4 all-gather.4
  267.6 32.3 reduce-scatter.4
where the time goes:
time: 312 us; the launch traced here: 308 us
  waiting for transfers between devices  191 us (61%)
  blocking collectives  73.8 us (24%)
  local copies, waits for them, and re-layouts  13.9 us (4%)
  between operations  13.9 us (4%)
  starting transfers between devices  7.38 us (2%)
  matrix products  5.61 us (2%)
    all_to_all x1, blocking collectives, body(): lax.all_to_all(layer_order(square_rows, row_count, layer_count), 'layer',...  58.3 us
    all_gather x1, waiting for transfers between devices, body(): full_rows = lax.all_gather(masked, 'col', axis=1, tiled=True)  45.4 us
    all_gather x1, waiting for transfers between devices, body(): square_rows = lax.all_gather(square, 'col', axis=1, tiled=True)  45.1 us
    reduce_scatter x1, waiting for transfers between devices, body(): lax.psum_scatter(square_terms, 'layer', scatter_dimension=0, tiled=True)  35.2 us
    all_to_all x1, waiting for transfers between devices, body(): lax.all_to_all(layer_order(full_rows, row_count, layer_count), 'layer', s...  32.8 us
    reduce_scatter x1, waiting for transfers between devices, body(): lax.psum_scatter(cube_terms, 'layer', scatter_dimension=0, tiled=True)  32.5 us
    all_gather x1, blocking collectives, body(): right_panel = lax.all_gather(masked, 'row', axis=0, tiled=True)  15.6 us
    all_to_all x1, starting transfers between devices, body(): lax.all_to_all(layer_order(full_rows, row_count, layer_count), 'layer', s...  7.23 us
  transfers between devices with their start and end apart: 5, of which 5 were waited for; matrix products, arithmetic and copies ran while one was open for 0% of the time, Pallas kernels for 0%

commit v1 on v0

v1 whole, which is shorter than its diff:
```python
import jax
import jax.numpy as jnp
from jax import lax
from jax.experimental import pallas as pl
from jax.experimental.pallas import tpu as pltpu
from jax.sharding import PartitionSpec as P

BLK = 128
SPAN = 4


def plane_permute(value, target):
    pairs = []
    for row in range(4):
        for x in range(4):
            for low in range(2):
                for core in range(2):
                    to = target(row, x, low, core)
                    pairs.append(
                        (
                            row * 16 + x * 4 + low * 2 + core,
                            to[0] * 16 + to[1] * 4 + to[2] * 2 + to[3],
                        )
                    )
    return lax.ppermute(value, ("row", "col"), pairs)


def split(value):
    high = value.astype(jnp.bfloat16)
    return high, (value - high.astype(jnp.float32)).astype(jnp.bfloat16)


def product_kernel(own_own, other_own, own_other, other_other, right, out):
    col = lax.axis_index("col")
    low, core = lax.rem(lax.div(col, 2), 2), lax.rem(col, 2)
    lefts = ((own_own, 0, 0), (other_own, 1, 0), (own_other, 0, 1), (other_other, 1, 1))
    rows = 4 * BLK
    total = jnp.zeros((rows, 256), jnp.float32)
    for ref, low_step, core_step in lefts:
        q = lax.rem(low + low_step, 2) * 2 + lax.rem(core + core_step, 2)
        left_high, left_low = split(ref[...].reshape(rows, 256))
        right_high, right_low = split(right[pl.ds(pl.multiple_of(q * 256, 256), 256), :])
        for a, b in ((left_high, right_high), (left_high, right_low), (left_low, right_high)):
            total = total + jnp.dot(a, b, preferred_element_type=jnp.float32)
    out[...] = total.reshape(4, BLK, 256)


def product(lefts, right):
    return pl.pallas_call(
        product_kernel,
        out_shape=jax.ShapeDtypeStruct((4, BLK, 256), jnp.float32),
        in_specs=[pl.BlockSpec(memory_space=pltpu.VMEM)] * 5,
        out_specs=pl.BlockSpec(memory_space=pltpu.VMEM),
        compiler_params=pltpu.CompilerParams(vmem_limit_bytes=32 * 1024 * 1024),
        cost_estimate=pl.CostEstimate(
            flops=6 * 512 * 1024 * 256, bytes_accessed=7 * 512 * 1024, transcendentals=0
        ),
    )(*lefts, right)


def body(density, pattern):
    row, col, layer = (lax.axis_index(name) for name in ("row", "col", "layer"))
    kept = lax.dynamic_slice(pattern, (row * 8 + layer, col * 2), (1, 2)).astype(jnp.float32)
    masked = density * jnp.repeat(kept, BLK, axis=1)
    right = lax.all_gather(masked, "layer").reshape(8 * BLK, 256)
    near = plane_permute(masked, lambda r, x, low, core: (x, r, low, core))
    far = plane_permute(masked, lambda r, x, low, core: (x, r, 1 - low, core))
    lines = [[x * SPAN + q for x in range(4)] for q in range(SPAN)]
    near_all = lax.all_gather(near, "col", axis_index_groups=lines)
    far_all = lax.all_gather(far, "col", axis_index_groups=lines)
    swap = [(i, i ^ 1) for i in range(16)]
    lefts = (
        near_all,
        far_all,
        lax.ppermute(near_all, "col", swap),
        lax.ppermute(far_all, "col", swap),
    )
    square_terms = product(lefts, right)
    square = jnp.sum(lax.all_to_all(square_terms, "row", 0, 0), axis=0)
    square_right = lax.all_to_all(
        jnp.broadcast_to(square[None], (8, BLK, 256)), "layer", 0, 0
    ).reshape(8 * BLK, 256)
    cube_terms = product(lefts, square_right)
    cube = jnp.sum(lax.all_to_all(cube_terms, "row", 0, 0), axis=0)
    return (square, 3.0 * square - 2.0 * cube)


def solution(mesh):
    in_specs = (P(("row", "layer"), "col"), P())
    out_specs = (P(("row", "layer"), "col"), P(("row", "layer"), "col"))
    return jax.shard_map(body, mesh=mesh, in_specs=in_specs, out_specs=out_specs, check_vma=False)
```

time: 312 us -> 153 us (0.49)
  the two profiles are of different devices: /device:TPU:1 before, /device:TPU:8 now
where the time goes in v1:
time: 153 us
  blocking collectives  115 us (75%)
  between operations  14.1 us (9%)
  starting transfers between devices  12.2 us (8%)
  waiting for transfers between devices  4.4 us (3%)
  other arithmetic  3.08 us (2%)
  local copies, waits for them, and re-layouts  2.27 us (1%)
  Pallas kernels  1.98 us (1%)
    all_to_all x1, blocking collectives, body(): lax.all_to_all(jnp.broadcast_to(square[None], (8, BLK, 256)), 'layer', 0, 0)  38.1 us
    all_to_all x1, blocking collectives, body(): square = jnp.sum(lax.all_to_all(square_terms, 'row', 0, 0), axis=0)  24.7 us
    all_gather x1, blocking collectives, body(): far_all = lax.all_gather(far, 'col', axis_index_groups=lines)  20.8 us
    all_to_all x1, blocking collectives, body(): cube = jnp.sum(lax.all_to_all(cube_terms, 'row', 0, 0), axis=0)  17.4 us
    all_gather x1, blocking collectives, body(): near_all = lax.all_gather(near, 'col', axis_index_groups=lines)  13.6 us
    ppermute x2, starting transfers between devices, plane_permute(): return lax.ppermute(value, ('row', 'col'), pairs)  8.39 us
  transfers between devices with their start and end apart: 5, of which 2 were waited for; matrix products, arithmetic and copies ran while one was open for 0% of the time, Pallas kernels for 0%

profile of v1, /device:TPU:8, one launch (start us, length us, event | category | flops | bytes accessed | tf_op | source)
XLA Modules:
  0.0 152.6 jit_solution(6284420461673066833)
XLA Ops:
  7.2 0.0 all-gather.5.cloned.1.call-start
  7.2 0.8 convert_bitcast_fusion
  8.0 0.1 broadcast_bitcast_fusion
  8.1 1.6 %broadcast_multiply_fusion = f32[128,256]{1,0:T(8,128)} fusion(f32[128,256]{1,0:T(8,128)} %param.2, f32[256]{0:T(256)S(1)} %broadcast_bitcast_fusion), kind=kLoop, calls=%fused_computation.1 | loop fusion | flops 32768 | bytes 263168 | tf_op jit(solution)/shard_map/mul | solution.py:64
  9.6 0.0 all-gather.5.cloned.1.call-update
  9.7 0.9 copy-done.2
  10.5 7.7 %collective-permute-start.1 = (f32[128,256]{1,0:T(8,128)S(1)}, f32[128,256]{1,0:T(8,128)S(1)}, u32[]{:S(2)}, u32[]{:S(2)}) collective-permute-start(f32[128,256]{1,0:T(8,128)S(1)} %copy-done.2), channel_id=1, source_target_pairs={{0,16},{8,24},{16,0},{24,8},{32,144},{40,152},{48,128},{56,136},{6... | collective-permute-start | bytes 393224 | tf_op jit(solution)/shard_map/ppermute | solution.py:25
  18.3 0.7 collective-permute-start
  18.9 2.5 %collective-permute-done.1 = f32[128,256]{1,0:T(8,128)S(1)} collective-permute-done((f32[128,256]{1,0:T(8,128)S(1)}, f32[128,256]{1,0:T(8,128)S(1)}, u32[]{:S(2)}, u32[]{:S(2)}) %collective-permute-start.1) | collective-permute-done | bytes 131104 | tf_op jit(solution)/shard_map/ppermute | solution.py:25
  21.4 20.8 %all-gather.1 = f32[512,256]{1,0:T(8,128)S(1)} all-gather(f32[128,256]{1,0:T(8,128)S(1)} %collective-permute-done.1), channel_id=3, replica_groups={{0,32,64,96},{8,40,72,104},{16,48,80,112},{24,56,88,120},{1,33,65,97},{..., dimensions={0}, use_global_device_ids=true | all-gather | bytes 655360 | tf_op jit(solution)/shard_map/all_gather | solution.py:70
  42.2 1.9 %collective-permute-start.3 = (f32[4,128,256]{2,1,0:T(8,128)S(1)}, f32[4,128,256]{2,1,0:T(8,128)S(1)}, u32[]{:S(2)}, u32[]{:S(2)}) collective-permute-start(f32[4,128,256]{2,1,0:T(8,128)S(1)} %bitcast.7), channel_id=1, source_target_pairs={{0,8},{8,0},{16,24},{24,16},{32,40},{40,32},{48,56},{56,48},{64,72... | collective-permute-start | bytes 1572872 | tf_op jit(solution)/shard_map/ppermute | solution.py:76
  44.1 13.6 %all-gather = f32[512,256]{1,0:T(8,128)S(1)} all-gather(f32[128,256]{1,0:T(8,128)S(1)} %collective-permute-done), channel_id=2, replica_groups={{0,32,64,96},{8,40,72,104},{16,48,80,112},{24,56,88,120},{1,33,65,97},{..., dimensions={0}, use_global_device_ids=true | all-gather | bytes 655360 | tf_op jit(solution)/shard_map/all_gather | solution.py:69
  57.7 1.9 %collective-permute-start.2 = (f32[4,128,256]{2,1,0:T(8,128)S(1)}, f32[4,128,256]{2,1,0:T(8,128)S(1)}, u32[]{:S(2)}, u32[]{:S(2)}) collective-permute-start(f32[4,128,256]{2,1,0:T(8,128)S(1)} %bitcast.10), channel_id=1, source_target_pairs={{0,8},{8,0},{16,24},{24,16},{32,40},{40,32},{48,56},{56,48},{64,72... | collective-permute-start | bytes 1572872 | tf_op jit(solution)/shard_map/ppermute | solution.py:75
  59.6 0.0 collective-permute-done.3.other_other
  59.7 1.9 %collective-permute-done.2.own_other = f32[4,128,256]{2,1,0:T(8,128)S(1)} collective-permute-done((f32[4,128,256]{2,1,0:T(8,128)S(1)}, f32[4,128,256]{2,1,0:T(8,128)S(1)}, u32[]{:S(2)}, u32[]{:S(2)}) %collective-permute-start.2) | collective-permute-done | bytes 524320 | tf_op jit(solution)/shard_map/ppermute | solution.py:75
  61.5 1.2 copy-done
  62.8 1.0 shard_map.41
  63.7 24.7 %all_to_all.15 = f32[4,128,256]{2,1,0:T(8,128)S(1)} all-to-all(f32[4,128,256]{2,1,0:T(8,128)S(1)} %shard_map.41), channel_id=1, replica_groups=mesh['row'=4,'col'=16,'layer'=8] {'row'}, dimensions={0} | all-to-all | bytes 1048576 | tf_op jit(solution)/shard_map/all_to_all | solution.py:79
  88.5 0.0 copy-start.1
  88.5 0.1 broadcast_in_dim.13
  88.6 38.1 %all_to_all.16 = f32[8,128,256]{2,1,0:T(8,128)S(1)} all-to-all(f32[8,128,256]{2,1,0:T(8,128)S(1)} %broadcast_in_dim.13), channel_id=1, replica_groups=mesh['row'=4,'col'=16,'layer'=8] {'layer'}, dimensions={0} | all-to-all | bytes 2097152 | tf_op jit(solution)/shard_map/all_to_all | solution.py:80
  126.6 1.0 shard_map.42
  127.6 17.4 %all_to_all.17 = f32[4,128,256]{2,1,0:T(8,128)S(1)} all-to-all(f32[4,128,256]{2,1,0:T(8,128)S(1)} %shard_map.42), channel_id=1, replica_groups=mesh['row'=4,'col'=16,'layer'=8] {'row'}, dimensions={0} | all-to-all | bytes 1048576 | tf_op jit(solution)/shard_map/all_to_all | solution.py:84
  145.1 0.7 multiply_subtract_fusion
  (7 shorter events, 0.1 us)
Async XLA Ops:
  7.2 54.4 %all-gather.5.cloned.1.call-start = ((), (), s32[]{:S(2)}) async-start(), calls=%async_computation.3 | async-start | bytes 1179648 | tf_op jit(solution)/shard_map/all_gather | solution.py:65
  9.6 0.9 copy-start.2
  10.5 10.9 %collective-permute-start.1 = (f32[128,256]{1,0:T(8,128)S(1)}, f32[128,256]{1,0:T(8,128)S(1)}, u32[]{:S(2)}, u32[]{:S(2)}) collective-permute-start(f32[128,256]{1,0:T(8,128)S(1)} %copy-done.2), channel_id=1, source_target_pairs={{0,16},{8,24},{16,0},{24,8},{32,144},{40,152},{48,128},{56,136},{6... | collective-permute-start | bytes 393224 | tf_op jit(solution)/shard_map/ppermute | solution.py:25
  18.3 25.9 %collective-permute-start = (f32[128,256]{1,0:T(8,128)S(1)}, f32[128,256]{1,0:T(8,128)S(1)}, u32[]{:S(2)}, u32[]{:S(2)}) collective-permute-start(f32[128,256]{1,0:T(8,128)S(1)} %copy-done.2), channel_id=1, source_target_pairs={{0,0},{8,8},{16,16},{24,24},{32,128},{40,136},{48,144},{56,152},{6... | collective-permute-start | bytes 393224 | tf_op jit(solution)/shard_map/ppermute | solution.py:25
  42.2 17.4 %collective-permute-start.3 = (f32[4,128,256]{2,1,0:T(8,128)S(1)}, f32[4,128,256]{2,1,0:T(8,128)S(1)}, u32[]{:S(2)}, u32[]{:S(2)}) collective-permute-start(f32[4,128,256]{2,1,0:T(8,128)S(1)} %bitcast.7), channel_id=1, source_target_pairs={{0,8},{8,0},{16,24},{24,16},{32,40},{40,32},{48,56},{56,48},{64,72... | collective-permute-start | bytes 1572872 | tf_op jit(solution)/shard_map/ppermute | solution.py:76
  57.7 3.8 %collective-permute-start.2 = (f32[4,128,256]{2,1,0:T(8,128)S(1)}, f32[4,128,256]{2,1,0:T(8,128)S(1)}, u32[]{:S(2)}, u32[]{:S(2)}) collective-permute-start(f32[4,128,256]{2,1,0:T(8,128)S(1)} %bitcast.10), channel_id=1, source_target_pairs={{0,8},{8,0},{16,24},{24,16},{32,40},{40,32},{48,56},{56,48},{64,72... | collective-permute-start | bytes 1572872 | tf_op jit(solution)/shard_map/ppermute | solution.py:75
  61.5 1.2 copy-start
  88.5 56.6 %copy-start.1 = (f32[128,256]{1,0:T(8,128)}, f32[128,256]{1,0:T(8,128)S(1)}, u32[]{:S(2)}) copy-start(f32[128,256]{1,0:T(8,128)S(1)} %reduce_sum.18) | copy-start | bytes 393220
Sparse Core Ops, SparseCore 0:
  10.7 46.7 all-gather.4

commit v2 on v1

v2 whole, which is shorter than its diff:
```python
import jax
import jax.numpy as jnp
from jax import lax
from jax.experimental import pallas as pl
from jax.experimental.pallas import tpu as pltpu
from jax.sharding import PartitionSpec as P

BLK = 128
WIDTH = 256
NEAR = 8


def split(value):
    high = value.astype(jnp.bfloat16)
    return high, (value - high.astype(jnp.float32)).astype(jnp.bfloat16)


def product_kernel(own, other, panel, out):
    core = lax.rem(lax.axis_index("col"), 2)
    total_high = jnp.zeros((2 * BLK, WIDTH), jnp.float32)
    total_low = jnp.zeros((BLK, WIDTH), jnp.float32)
    for ref, core_step in ((own, 0), (other, 1)):
        q_core = lax.rem(core + core_step, 2)
        for low in range(2):
            for x in range(4):
                left_high, left_low = split(ref[x * 2 + low])
                right = panel[pl.ds(4 * low + 2 * q_core, 2), x].reshape(2 * BLK, WIDTH)
                right_high, right_low = split(right)
                both = jnp.concatenate([left_high, left_low], axis=0)
                total_high += jnp.dot(both, right_high, preferred_element_type=jnp.float32)
                total_low += jnp.dot(left_high, right_low, preferred_element_type=jnp.float32)
    out[...] = total_high[:BLK] + (total_high[BLK:] + total_low)


def product(own, other, panel):
    return pl.pallas_call(
        product_kernel,
        out_shape=jax.ShapeDtypeStruct((BLK, WIDTH), jnp.float32),
        in_specs=[pl.BlockSpec(memory_space=pltpu.VMEM)] * 3,
        out_specs=pl.BlockSpec(memory_space=pltpu.VMEM),
        compiler_params=pltpu.CompilerParams(vmem_limit_bytes=32 * 1024 * 1024),
        cost_estimate=pl.CostEstimate(
            flops=6 * BLK * 4096 * WIDTH, bytes_accessed=6 * 1024 * 1024, transcendentals=0
        ),
    )(own, other, panel)


def slab(block):
    groups = [[chip * 2 + core for chip in range(NEAR)] for core in range(2)]
    copies = jnp.broadcast_to(block[None], (NEAR, BLK, WIDTH))
    own = lax.all_to_all(copies, "col", 0, 0, axis_index_groups=groups)
    return own, lax.ppermute(own, "col", [(i, i ^ 1) for i in range(16)])


def body(density, pattern):
    row, col, layer = (lax.axis_index(name) for name in ("row", "col", "layer"))
    kept = lax.dynamic_slice(pattern, (row * 8 + layer, col * 2), (1, 2)).astype(jnp.float32)
    masked = density * jnp.repeat(kept, BLK, axis=1)
    panel = lax.all_gather(lax.all_gather(masked, "row"), "layer")
    square = product(*slab(masked), panel)
    cube = product(*slab(square), panel)
    return (square, 3.0 * square - 2.0 * cube)


def solution(mesh):
    in_specs = (P(("row", "layer"), "col"), P())
    out_specs = (P(("row", "layer"), "col"), P(("row", "layer"), "col"))
    return jax.shard_map(body, mesh=mesh, in_specs=in_specs, out_specs=out_specs, check_vma=False)
```

time: 153 us -> 130 us (0.85)
  the two profiles are of different devices: /device:TPU:8 before, /device:TPU:1 now
where the time goes in v2:
time: 130 us; the launch traced here: 129 us
  blocking collectives  52.3 us (40%)
  waiting for transfers between devices  43.4 us (33%)
  between operations  14.1 us (11%)
  starting transfers between devices  11.1 us (9%)
  local copies, waits for them, and re-layouts  3.34 us (3%)
  Pallas kernels  2.77 us (2%)
  other arithmetic  2.35 us (2%)
    all_gather x1, waiting for transfers between devices, body(): panel = lax.all_gather(lax.all_gather(masked, 'row'), 'layer')  38.9 us
    all_to_all x2, blocking collectives, slab(): own = lax.all_to_all(copies, 'col', 0, 0, axis_index_groups=groups)  34.7 us
    all_gather x1, blocking collectives, body(): panel = lax.all_gather(lax.all_gather(masked, 'row'), 'layer')  17.6 us
    ppermute x2, starting transfers between devices, slab(): return (own, lax.ppermute(own, 'col', [(i, i ^ 1) for i in range(16)]))  11.1 us
    ppermute x2, waiting for transfers between devices, slab(): return (own, lax.ppermute(own, 'col', [(i, i ^ 1) for i in range(16)]))  4.53 us
    pallas_call x2, Pallas kernels, product(): pl.pallas_call(product_kernel, out_shape=jax.ShapeDtypeStruct((BLK, WIDTH...  2.77 us
  transfers between devices with their start and end apart: 3, of which 3 were waited for; matrix products, arithmetic and copies ran while one was open for 0% of the time, Pallas kernels for 0%

profile of v2, /device:TPU:1, one launch (start us, length us, event | category | flops | bytes accessed | tf_op | source)
XLA Modules:
  0.0 129.4 jit_solution(15391937941062038898)
XLA Ops:
  7.2 0.0 all-gather.4.cloned.1.call-start
  7.2 0.8 convert_bitcast_fusion
  8.0 0.1 broadcast_bitcast_fusion
  8.1 0.9 broadcast_multiply_fusion
  9.0 17.6 %all-gather = f32[512,256]{1,0:T(8,128)} all-gather(f32[128,256]{1,0:T(8,128)S(1)} %broadcast_multiply_fusion), channel_id=2, replica_groups=mesh['row'=4,'col'=16,'layer'=8] {'row'}, dimensions={0}, use_global_device_ids=true | all-gather | bytes 655360 | tf_op jit(solution)/shard_map/all_gather | solution.py:59
  26.6 0.0 all-gather.4.cloned.1.call-update
  26.6 0.1 broadcast_in_dim.21
  26.7 15.0 %all_to_all.10.own = f32[8,128,256]{2,1,0:T(8,128)S(1)} all-to-all(f32[8,128,256]{2,1,0:T(8,128)S(1)} %broadcast_in_dim.21), channel_id=1, replica_groups={{0,16,32,48,64,80,96,112},{8,24,40,56,72,88,104,120},{1,17,33,49,65,81,..., dimensions={0} | all-to-all | bytes 2097152 | tf_op jit(solution)/shard_map/all_to_all | solution.py:51
  41.7 7.3 %collective-permute-start = (f32[8,128,256]{2,1,0:T(8,128)S(1)}, f32[8,128,256]{2,1,0:T(8,128)S(1)}, u32[]{:S(2)}, u32[]{:S(2)}) collective-permute-start(f32[8,128,256]{2,1,0:T(8,128)S(1)} %all_to_all.10.own), channel_id=1, source_target_pairs={{0,8},{8,0},{16,24},{24,16},{32,40},{40,32},{48,56},{56,48},{64,72... | collective-permute-start | bytes 3145736 | tf_op jit(solution)/shard_map/ppermute | solution.py:52
  49.0 2.3 %collective-permute-done.other = f32[8,128,256]{2,1,0:T(8,128)S(1)} collective-permute-done((f32[8,128,256]{2,1,0:T(8,128)S(1)}, f32[8,128,256]{2,1,0:T(8,128)S(1)}, u32[]{:S(2)}, u32[]{:S(2)}) %collective-permute-start) | collective-permute-done | bytes 1048608 | tf_op jit(solution)/shard_map/ppermute | solution.py:52
  51.2 38.9 %all-gather.4.cloned.1.call-done = f32[32,128,256]{2,1,0:T(8,128)} async-done(((f32[4,128,256]{2,1,0:T(8,128)}), f32[32,128,256]{2,1,0:T(8,128)}) %all-gather.4.cloned.1.call-update) | async-done | bytes 4194320 | tf_op jit(solution)/shard_map/all_gather | solution.py:59
  90.1 0.0 copy-start
  90.1 2.2 %copy-done = f32[32,128,256]{2,1,0:T(8,128)S(1)} copy-done((f32[32,128,256]{2,1,0:T(8,128)S(1)}, f32[32,128,256]{2,1,0:T(8,128)}, u32[]{:S(2)}) %copy-start) | copy-done | bytes 4194328
  92.3 0.0 copy-start.1
  92.3 1.7 %shard_map.41 = f32[128,256]{1,0:T(8,128)} custom-call(f32[8,128,256]{2,1,0:T(8,128)S(1)} %all_to_all.10.own, f32[8,128,256]{2,1,0:T(8,128)S(1)} %collective-permute-done.other, f32[8,4,128,256]{3,2,1,0:T(8,128)S(1)} %bitcast.6), custom_call_target="tpu_custom_call" | custom-call | flops 805306368 | bytes 6291456 | tf_op jit(solution)/shard_map/pallas_call | solution.py:36
  94.0 1.0 broadcast_in_dim.23
  95.0 0.0 copy-start.2
  95.0 19.7 %all_to_all.11.own = f32[8,128,256]{2,1,0:T(8,128)S(1)} all-to-all(f32[8,128,256]{2,1,0:T(8,128)S(1)} %broadcast_in_dim.23), channel_id=1, replica_groups={{0,16,32,48,64,80,96,112},{8,24,40,56,72,88,104,120},{1,17,33,49,65,81,..., dimensions={0} | all-to-all | bytes 2097152 | tf_op jit(solution)/shard_map/all_to_all | solution.py:51
  114.8 3.8 %collective-permute-start.1 = (f32[8,128,256]{2,1,0:T(8,128)S(1)}, f32[8,128,256]{2,1,0:T(8,128)S(1)}, u32[]{:S(2)}, u32[]{:S(2)}) collective-permute-start(f32[8,128,256]{2,1,0:T(8,128)S(1)} %all_to_all.11.own), channel_id=1, source_target_pairs={{0,8},{8,0},{16,24},{24,16},{32,40},{40,32},{48,56},{56,48},{64,72... | collective-permute-start | bytes 3145736 | tf_op jit(solution)/shard_map/ppermute | solution.py:52
  118.5 2.3 %collective-permute-done.1.other = f32[8,128,256]{2,1,0:T(8,128)S(1)} collective-permute-done((f32[8,128,256]{2,1,0:T(8,128)S(1)}, f32[8,128,256]{2,1,0:T(8,128)S(1)}, u32[]{:S(2)}, u32[]{:S(2)}) %collective-permute-start.1) | collective-permute-done | bytes 1048608 | tf_op jit(solution)/shard_map/ppermute | solution.py:52
  120.8 0.0 copy-done.1
  120.8 1.1 shard_map.42
  121.9 0.0 copy-done.2
  121.9 0.7 multiply_subtract_fusion
Async XLA Ops:
  7.2 82.9 %all-gather.4.cloned.1.call-start = ((), (), s32[]{:S(2)}) async-start(), calls=%async_computation.2 | async-start | bytes 4718592 | tf_op jit(solution)/shard_map/all_gather | solution.py:59
  41.7 9.6 %collective-permute-start = (f32[8,128,256]{2,1,0:T(8,128)S(1)}, f32[8,128,256]{2,1,0:T(8,128)S(1)}, u32[]{:S(2)}, u32[]{:S(2)}) collective-permute-start(f32[8,128,256]{2,1,0:T(8,128)S(1)} %all_to_all.10.own), channel_id=1, source_target_pairs={{0,8},{8,0},{16,24},{24,16},{32,40},{40,32},{48,56},{56,48},{64,72... | collective-permute-start | bytes 3145736 | tf_op jit(solution)/shard_map/ppermute | solution.py:52
  90.1 2.2 %copy-start = (f32[32,128,256]{2,1,0:T(8,128)S(1)}, f32[32,128,256]{2,1,0:T(8,128)}, u32[]{:S(2)}) copy-start(f32[32,128,256]{2,1,0:T(8,128)} %all-gather.4.cloned.1.call-done) | copy-start | bytes 12582916
  92.3 28.5 %copy-start.1 = (f32[32,128,256]{2,1,0:T(8,128)S(1)}, f32[32,128,256]{2,1,0:T(8,128)}, u32[]{:S(2)}) copy-start(f32[32,128,256]{2,1,0:T(8,128)} %all-gather.4.cloned.1.call-done) | copy-start | bytes 12582916
  95.0 26.9 %copy-start.2 = (f32[128,256]{1,0:T(8,128)S(1)}, f32[128,256]{1,0:T(8,128)}, u32[]{:S(2)}) copy-start(f32[128,256]{1,0:T(8,128)} %shard_map.41) | copy-start | bytes 393220
  114.8 6.0 %collective-permute-start.1 = (f32[8,128,256]{2,1,0:T(8,128)S(1)}, f32[8,128,256]{2,1,0:T(8,128)S(1)}, u32[]{:S(2)}, u32[]{:S(2)}) collective-permute-start(f32[8,128,256]{2,1,0:T(8,128)S(1)} %all_to_all.11.own), channel_id=1, source_target_pairs={{0,8},{8,0},{16,24},{24,16},{32,40},{40,32},{48,56},{56,48},{64,72... | collective-permute-start | bytes 3145736 | tf_op jit(solution)/shard_map/ppermute | solution.py:52
Sparse Core Ops, SparseCore 0:
  26.7 63.3 all-gather.3

commit v3 on v2

v3 whole, which is shorter than its diff:
```python
import jax
import jax.numpy as jnp
from jax import lax
from jax.experimental import pallas as pl
from jax.experimental.pallas import tpu as pltpu
from jax.sharding import PartitionSpec as P

BLK = 128
HALF = 64
WIDTH = 256
ROWS = 4
NEAR = 8
LAYERS = 8


def split(value):
    high = value.astype(jnp.bfloat16)
    return high, (value - high.astype(jnp.float32)).astype(jnp.bfloat16)


def triple_dot(left, right, dims):
    left_high, left_low = split(left)
    right_high, right_low = split(right)
    total = lax.dot_general(left_high, right_low, dims, preferred_element_type=jnp.float32)
    total += lax.dot_general(left_low, right_high, dims, preferred_element_type=jnp.float32)
    return total + lax.dot_general(left_high, right_high, dims, preferred_element_type=jnp.float32)


def first_kernel(rows, own, other, out):
    left_own = rows[:, 0].reshape(ROWS * HALF, WIDTH)
    left_other = rows[:, 1].reshape(ROWS * HALF, WIDTH)
    dims = (((1,), (1,)), ((), ()))
    for pair in range(LAYERS // 2):
        span = pl.ds(pair * 2 * BLK, 2 * BLK)
        total = triple_dot(left_own, own[span, :], dims)
        total += triple_dot(left_other, other[span, :], dims)
        out[2 * pair] = total[:, :BLK]
        out[2 * pair + 1] = total[:, BLK:]


def second_kernel(square, own, other, out):
    dims = (((1,), (0,)), ((), ()))
    for side, panel in ((0, own), (1, other)):
        total = jnp.zeros((ROWS * HALF, WIDTH), jnp.float32)
        for pair in range(LAYERS // 2):
            left = jnp.concatenate([square[2 * pair], square[2 * pair + 1]], axis=1)
            total += triple_dot(left, panel[pl.ds(pair * 2 * BLK, 2 * BLK), :], dims)
        for row in range(ROWS):
            out[row, side] = total[row * HALF : (row + 1) * HALF]


def call(kernel, shape, *operands):
    return pl.pallas_call(
        kernel,
        out_shape=jax.ShapeDtypeStruct(shape, jnp.float32),
        in_specs=[pl.BlockSpec(memory_space=pltpu.VMEM)] * len(operands),
        out_specs=pl.BlockSpec(memory_space=pltpu.VMEM),
        compiler_params=pltpu.CompilerParams(vmem_limit_bytes=32 * 1024 * 1024),
        cost_estimate=pl.CostEstimate(
            flops=6 * 256 * 512 * 1024, bytes_accessed=4 * 1024 * 1024, transcendentals=0
        ),
    )(*operands)


def swap_core(value):
    return lax.ppermute(value, "col", [(i, i ^ 1) for i in range(16)])


def mirror_chunk(piece, turn, core, layer):
    pairs = []
    for r in range(4):
        for c in range(16):
            for z in range(LAYERS):
                i = 2 * (c % 2) + (z + turn) % 2
                to = (r * 16 + i * 4 + z // 2) * LAYERS + c // 2
                pairs.append(((r * 16 + c) * LAYERS + z, to))
    chunk = lax.dynamic_index_in_dim(piece, (layer + turn) % 2, 0, keepdims=False)
    return lax.ppermute(chunk, ("row", "col", "layer"), pairs)


def near_exchange(value):
    groups = [[chip * 2 + core for chip in range(NEAR)] for core in range(2)]
    return lax.all_to_all(value, "col", 0, 0, axis_index_groups=groups)


def copies(value, count):
    return jnp.broadcast_to(value[None], (count, *value.shape))


def join_halves(mine, received, core):
    low = jnp.where(core == 0, mine, received)
    high = jnp.where(core == 0, received, mine)
    return jnp.concatenate([low, high], axis=0)


def body(density, pattern):
    row, col, layer = (lax.axis_index(name) for name in ("row", "col", "layer"))
    x, core = col // 4, col % 2
    kept = lax.dynamic_slice(pattern, (row * 8 + layer, col * 2), (1, 2)).astype(jnp.float32)
    masked = density * jnp.repeat(kept, BLK, axis=1)

    own = lax.all_to_all(copies(masked, LAYERS), "layer", 0, 0).reshape(LAYERS * BLK, WIDTH)

    halves = masked.reshape(2, HALF, WIDTH)
    mine = lax.dynamic_index_in_dim(halves, core, 0, keepdims=False)
    theirs = lax.dynamic_index_in_dim(halves, 1 - core, 0, keepdims=False)
    rows = jnp.concatenate([mine, swap_core(theirs)], axis=0)
    rows = lax.all_gather(rows, "row").reshape(ROWS, 2, HALF, WIDTH)

    own, rows = lax.optimization_barrier((own, rows))
    other = swap_core(own)
    square_terms = call(first_kernel, (LAYERS, ROWS * HALF, BLK), rows, own, other)
    square_piece = jnp.sum(near_exchange(square_terms), axis=0)
    square_rows = near_exchange(copies(square_piece, NEAR))

    pieces = square_piece.reshape(2, 2, HALF, BLK)
    mine = lax.dynamic_index_in_dim(pieces, core, 0, keepdims=False)
    theirs = swap_core(lax.dynamic_index_in_dim(pieces, 1 - core, 0, keepdims=False))
    pieces = jnp.where(
        core == 0,
        jnp.concatenate([mine, theirs], axis=1),
        jnp.concatenate([theirs, mine], axis=1),
    )
    square_rows, pieces = lax.optimization_barrier((square_rows, pieces))
    first = mirror_chunk(pieces, 0, core, layer)
    second = mirror_chunk(pieces, 1, core, layer)

    cube_terms = call(second_kernel, (ROWS, 2, HALF, WIDTH), square_rows, own, other)
    cube = jnp.sum(lax.all_to_all(cube_terms, "row", 0, 0), axis=0)
    cube, first, second = lax.optimization_barrier((cube, first, second))
    cube_home = join_halves(cube[0], swap_core(cube[1]), core)

    even = x % 2 == 0
    square_home = jnp.concatenate(
        [jnp.where(even, first, second).T, jnp.where(even, second, first).T], axis=1
    )
    return (square_home, 3.0 * square_home - 2.0 * cube_home)


def solution(mesh):
    in_specs = (P(("row", "layer"), "col"), P())
    out_specs = (P(("row", "layer"), "col"), P(("row", "layer"), "col"))
    return jax.shard_map(body, mesh=mesh, in_specs=in_specs, out_specs=out_specs, check_vma=False)
```

time: 130 us -> 121 us (0.931)
  the two profiles are of different devices: /device:TPU:1 before, /device:TPU:107 now
where the time goes in v3:
time: 121 us
  starting transfers between devices  42.3 us (35%)
  waiting for transfers between devices  37 us (31%)
  blocking collectives  32 us (26%)
  other arithmetic  3.64 us (3%)
  local copies, waits for them, and re-layouts  3.19 us (3%)
  Pallas kernels  2.01 us (2%)
    all_to_all x1, blocking collectives, near_exchange(): return lax.all_to_all(value, 'col', 0, 0, axis_index_groups=groups)  18.7 us
    ppermute x2, waiting for transfers between devices, mirror_chunk(): return lax.ppermute(chunk, ('row', 'col', 'layer'), pairs)  16 us
    ppermute x4, starting transfers between devices, swap_core(): return lax.ppermute(value, 'col', [(i, i ^ 1) for i in range(16)])  13.7 us
    all_gather x1, blocking collectives, body(): rows = lax.all_gather(rows, 'row').reshape(ROWS, 2, HALF, WIDTH)  13.4 us
    all_to_all x1, starting transfers between devices, body(): lax.all_to_all(copies(masked, LAYERS), 'layer', 0, 0)  9.4 us
    all_to_all x1, waiting for transfers between devices, body(): lax.all_to_all(copies(masked, LAYERS), 'layer', 0, 0)  8.41 us
    ppermute x2, starting transfers between devices, mirror_chunk(): return lax.ppermute(chunk, ('row', 'col', 'layer'), pairs)  7.98 us
    all_to_all x1, waiting for transfers between devices, near_exchange(): return lax.all_to_all(value, 'col', 0, 0, axis_index_groups=groups)  7.18 us
  transfers between devices with their start and end apart: 9, of which 8 were waited for; matrix products, arithmetic and copies ran while one was open for 1% of the time, Pallas kernels for 0%

profile of v3, /device:TPU:107, one launch (start us, length us, event | category | flops | bytes accessed | tf_op | source)
XLA Modules:
  0.0 120.9 jit_solution(14563252121249405474)
XLA Ops:
  1.5 0.9 broadcast_multiply_fusion
  2.4 1.1 broadcast_in_dim.19
  3.5 9.4 %all-to-all-start = ((f32[8,128,256]{2,1,0:T(8,128)}), f32[8,128,256]{2,1,0:T(8,128)S(1)}, u32[]{:S(2)}, u32[]{:S(2)}) async-start(f32[8,128,256]{2,1,0:T(8,128)} %broadcast_in_dim.19), calls=%async_computation | async-start | bytes 2097152 | tf_op jit(solution)/shard_map/all_to_all | solution.py:102
  12.9 3.1 %collective-permute-start = (f32[64,256]{1,0:T(8,128)S(1)}, f32[64,256]{1,0:T(8,128)S(1)}, u32[]{:S(2)}, u32[]{:S(2)}) collective-permute-start(f32[64,256]{1,0:T(8,128)S(1)} %get-tuple-element.27), channel_id=1, source_target_pairs={{0,8},{8,0},{16,24},{24,16},{32,40},{40,32},{48,56},{56,48},{64,72... | collective-permute-start | bytes 196616 | tf_op jit(solution)/shard_map/ppermute | solution.py:66
  16.9 13.4 %all-gather = f32[512,256]{1,0:T(8,128)S(1)} all-gather(f32[128,256]{1,0:T(8,128)S(1)} %pad_maximum_fusion), channel_id=2, replica_groups=mesh['row'=4,'col'=16,'layer'=8] {'row'}, dimensions={0}, use_global_device_ids=true | all-gather | bytes 655360 | tf_op jit(solution)/shard_map/all_gather | solution.py:108
  30.3 8.4 %all-to-all-done = f32[8,128,256]{2,1,0:T(8,128)S(1)} async-done(((f32[8,128,256]{2,1,0:T(8,128)}), f32[8,128,256]{2,1,0:T(8,128)S(1)}, u32[]{:S(2)}, u32[]{:S(2)}) %all-to-all-start) | async-done | bytes 1048608 | tf_op jit(solution)/shard_map/all_to_all | solution.py:102
  38.7 4.6 %collective-permute-start.1 = (f32[1024,256]{1,0:T(8,128)S(1)}, f32[1024,256]{1,0:T(8,128)S(1)}, u32[]{:S(2)}, u32[]{:S(2)}) collective-permute-start(f32[1024,256]{1,0:T(8,128)S(1)} %bitcast.27), channel_id=1, source_target_pairs={{0,8},{8,0},{16,24},{24,16},{32,40},{40,32},{48,56},{56,48},{64,72... | collective-permute-start | bytes 3145736 | tf_op jit(solution)/shard_map/ppermute | solution.py:66
  43.3 2.3 %collective-permute-done.1.other = f32[1024,256]{1,0:T(8,128)S(1)} collective-permute-done((f32[1024,256]{1,0:T(8,128)S(1)}, f32[1024,256]{1,0:T(8,128)S(1)}, u32[]{:S(2)}, u32[]{:S(2)}) %collective-permute-start.1) | collective-permute-done | bytes 1048608 | tf_op jit(solution)/shard_map/ppermute | solution.py:66
  45.5 1.0 shard_map.41
  46.6 18.7 %all_to_all.20 = f32[8,256,128]{2,1,0:T(8,128)S(1)} all-to-all(f32[8,256,128]{2,1,0:T(8,128)S(1)} %shard_map.41), channel_id=1, replica_groups={{0,16,32,48,64,80,96,112},{8,24,40,56,72,88,104,120},{1,17,33,49,65,81,..., dimensions={0} | all-to-all | bytes 2097152 | tf_op jit(solution)/shard_map/all_to_all | solution.py:83
  65.3 1.0 broadcast_in_dim.20
  66.3 4.6 %all-to-all-start.2 = ((f32[8,256,128]{2,1,0:T(8,128)}), f32[8,256,128]{2,1,0:T(8,128)S(1)}, u32[]{:S(2)}, u32[]{:S(2)}) async-start(f32[8,256,128]{2,1,0:T(8,128)} %broadcast_in_dim.20), calls=%async_computation.2 | async-start | bytes 2097152 | tf_op jit(solution)/shard_map/all_to_all | solution.py:83
  71.1 4.0 %collective-permute-start.2 = (f32[2,64,128]{1,2,0:T(8,128)S(1)}, f32[2,64,128]{1,2,0:T(8,128)}, u32[]{:S(2)}, u32[]{:S(2)}) collective-permute-start(f32[2,64,128]{1,2,0:T(8,128)S(1)} %bitcast.34), channel_id=1, source_target_pairs={{0,8},{8,0},{16,24},{24,16},{32,40},{40,32},{48,56},{56,48},{64,72... | collective-permute-start | bytes 196616 | tf_op jit(solution)/shard_map/ppermute | solution.py:66
  75.2 1.0 collective-permute-done.2
  76.2 1.1 maximum_select_fusion
  77.3 7.2 %all-to-all-done.2.square = f32[8,256,128]{2,1,0:T(8,128)S(1)} async-done(((f32[8,256,128]{2,1,0:T(8,128)}), f32[8,256,128]{2,1,0:T(8,128)S(1)}, u32[]{:S(2)}, u32[]{:S(2)}) %all-to-all-start.2) | async-done | bytes 1048608 | tf_op jit(solution)/shard_map/all_to_all | solution.py:83
  84.5 1.0 shard_map.42
  86.3 6.6 %all-to-all-start.3 = ((f32[4,2,64,256]{3,2,1,0:T(8,128)}), f32[4,2,64,256]{3,2,1,0:T(8,128)S(1)}, u32[]{:S(2)}, u32[]{:S(2)}) async-start(f32[4,2,64,256]{3,2,1,0:T(8,128)} %copy-done), calls=%async_computation.3 | async-start | bytes 1048576 | tf_op jit(solution)/shard_map/all_to_all | solution.py:129
  92.9 3.1 %collective-permute-start.4 = (f32[128,128]{0,1:T(8,128)S(1)}, f32[128,128]{0,1:T(8,128)S(1)}, u32[]{:S(2)}, u32[]{:S(2)}) collective-permute-start(f32[128,128]{0,1:T(8,128)S(1)} %get-tuple-element.22), channel_id=1, source_target_pairs={{0,32},{1,0},{2,40},{3,8},{4,48},{5,16},{6,56},{7,24},{8,96},{9,64... | collective-permute-start | bytes 196616 | tf_op jit(solution)/shard_map/ppermute | solution.py:78
  96.1 4.9 %collective-permute-start.3 = (f32[128,128]{0,1:T(8,128)S(1)}, f32[128,128]{0,1:T(8,128)S(1)}, u32[]{:S(2)}, u32[]{:S(2)}) collective-permute-start(f32[128,128]{0,1:T(8,128)S(1)} %get-tuple-element.23), channel_id=1, source_target_pairs={{0,0},{1,32},{2,8},{3,40},{4,16},{5,48},{6,24},{7,56},{8,64},{9,96... | collective-permute-start | bytes 196616 | tf_op jit(solution)/shard_map/ppermute | solution.py:78
  101.0 2.5 %collective-permute-done.4 = f32[128,128]{0,1:T(8,128)S(1)} collective-permute-done((f32[128,128]{0,1:T(8,128)S(1)}, f32[128,128]{0,1:T(8,128)S(1)}, u32[]{:S(2)}, u32[]{:S(2)}) %collective-permute-start.4) | collective-permute-done | bytes 65568 | tf_op jit(solution)/shard_map/ppermute | solution.py:78
  103.5 13.5 %collective-permute-done.3 = f32[128,128]{0,1:T(8,128)S(1)} collective-permute-done((f32[128,128]{0,1:T(8,128)S(1)}, f32[128,128]{0,1:T(8,128)S(1)}, u32[]{:S(2)}, u32[]{:S(2)}) %collective-permute-start.3) | collective-permute-done | bytes 65568 | tf_op jit(solution)/shard_map/ppermute | solution.py:78
  117.1 1.9 %collective-permute-start.5 = (f32[64,256]{1,0:T(8,128)S(1)}, f32[64,256]{1,0:T(8,128)S(1)}, u32[]{:S(2)}, u32[]{:S(2)}) collective-permute-start(f32[64,256]{1,0:T(8,128)S(1)} %slice_bitcast_fusion), channel_id=1, source_target_pairs={{0,8},{8,0},{16,24},{24,16},{32,40},{40,32},{48,56},{56,48},{64,72... | collective-permute-start | bytes 196616 | tf_op jit(solution)/shard_map/ppermute | solution.py:66
  119.0 1.2 collective-permute-done.5
  (18 shorter events, 3.6 us)
Async XLA Ops:
  3.5 35.2 %all-to-all-start = ((f32[8,128,256]{2,1,0:T(8,128)}), f32[8,128,256]{2,1,0:T(8,128)S(1)}, u32[]{:S(2)}, u32[]{:S(2)}) async-start(f32[8,128,256]{2,1,0:T(8,128)} %broadcast_in_dim.19), calls=%async_computation | async-start | bytes 2097152 | tf_op jit(solution)/shard_map/all_to_all | solution.py:102
  12.9 4.0 %collective-permute-start = (f32[64,256]{1,0:T(8,128)S(1)}, f32[64,256]{1,0:T(8,128)S(1)}, u32[]{:S(2)}, u32[]{:S(2)}) collective-permute-start(f32[64,256]{1,0:T(8,128)S(1)} %get-tuple-element.27), channel_id=1, source_target_pairs={{0,8},{8,0},{16,24},{24,16},{32,40},{40,32},{48,56},{56,48},{64,72... | collective-permute-start | bytes 196616 | tf_op jit(solution)/shard_map/ppermute | solution.py:66
  38.7 6.9 %collective-permute-start.1 = (f32[1024,256]{1,0:T(8,128)S(1)}, f32[1024,256]{1,0:T(8,128)S(1)}, u32[]{:S(2)}, u32[]{:S(2)}) collective-permute-start(f32[1024,256]{1,0:T(8,128)S(1)} %bitcast.27), channel_id=1, source_target_pairs={{0,8},{8,0},{16,24},{24,16},{32,40},{40,32},{48,56},{56,48},{64,72... | collective-permute-start | bytes 3145736 | tf_op jit(solution)/shard_map/ppermute | solution.py:66
  66.3 18.2 %all-to-all-start.2 = ((f32[8,256,128]{2,1,0:T(8,128)}), f32[8,256,128]{2,1,0:T(8,128)S(1)}, u32[]{:S(2)}, u32[]{:S(2)}) async-start(f32[8,256,128]{2,1,0:T(8,128)} %broadcast_in_dim.20), calls=%async_computation.2 | async-start | bytes 2097152 | tf_op jit(solution)/shard_map/all_to_all | solution.py:83
  71.1 5.1 %collective-permute-start.2 = (f32[2,64,128]{1,2,0:T(8,128)S(1)}, f32[2,64,128]{1,2,0:T(8,128)}, u32[]{:S(2)}, u32[]{:S(2)}) collective-permute-start(f32[2,64,128]{1,2,0:T(8,128)S(1)} %bitcast.34), channel_id=1, source_target_pairs={{0,8},{8,0},{16,24},{24,16},{32,40},{40,32},{48,56},{56,48},{64,72... | collective-permute-start | bytes 196616 | tf_op jit(solution)/shard_map/ppermute | solution.py:66
  85.5 0.8 copy-start
  86.3 14.7 %all-to-all-start.3 = ((f32[4,2,64,256]{3,2,1,0:T(8,128)}), f32[4,2,64,256]{3,2,1,0:T(8,128)S(1)}, u32[]{:S(2)}, u32[]{:S(2)}) async-start(f32[4,2,64,256]{3,2,1,0:T(8,128)} %copy-done), calls=%async_computation.3 | async-start | bytes 1048576 | tf_op jit(solution)/shard_map/all_to_all | solution.py:129
  92.9 10.6 %collective-permute-start.4 = (f32[128,128]{0,1:T(8,128)S(1)}, f32[128,128]{0,1:T(8,128)S(1)}, u32[]{:S(2)}, u32[]{:S(2)}) collective-permute-start(f32[128,128]{0,1:T(8,128)S(1)} %get-tuple-element.22), channel_id=1, source_target_pairs={{0,32},{1,0},{2,40},{3,8},{4,48},{5,16},{6,56},{7,24},{8,96},{9,64... | collective-permute-start | bytes 196616 | tf_op jit(solution)/shard_map/ppermute | solution.py:78
  96.1 21.0 %collective-permute-start.3 = (f32[128,128]{0,1:T(8,128)S(1)}, f32[128,128]{0,1:T(8,128)S(1)}, u32[]{:S(2)}, u32[]{:S(2)}) collective-permute-start(f32[128,128]{0,1:T(8,128)S(1)} %get-tuple-element.23), channel_id=1, source_target_pairs={{0,0},{1,32},{2,8},{3,40},{4,16},{5,48},{6,24},{7,56},{8,64},{9,96... | collective-permute-start | bytes 196616 | tf_op jit(solution)/shard_map/ppermute | solution.py:78
  117.1 3.1 %collective-permute-start.5 = (f32[64,256]{1,0:T(8,128)S(1)}, f32[64,256]{1,0:T(8,128)S(1)}, u32[]{:S(2)}, u32[]{:S(2)}) collective-permute-start(f32[64,256]{1,0:T(8,128)S(1)} %slice_bitcast_fusion), channel_id=1, source_target_pairs={{0,8},{8,0},{16,24},{24,16},{32,40},{40,32},{48,56},{56,48},{64,72... | collective-permute-start | bytes 196616 | tf_op jit(solution)/shard_map/ppermute | solution.py:66

commit v4 on v3

v4 whole, which is shorter than its diff:
```python
import jax
import jax.numpy as jnp
from jax import lax
from jax.experimental import pallas as pl
from jax.experimental.pallas import tpu as pltpu
from jax.sharding import PartitionSpec as P

BLK = 128
HALF = 64
WIDTH = 256
ROWS = 4
NEAR = 8
LAYERS = 8


def split(value):
    high = value.astype(jnp.bfloat16)
    return high, (value - high.astype(jnp.float32)).astype(jnp.bfloat16)


def triple_dot(left, right, dims):
    left_high, left_low = split(left)
    right_high, right_low = split(right)
    total = lax.dot_general(left_high, right_low, dims, preferred_element_type=jnp.float32)
    total += lax.dot_general(left_low, right_high, dims, preferred_element_type=jnp.float32)
    return total + lax.dot_general(left_high, right_high, dims, preferred_element_type=jnp.float32)


def first_kernel(rows, own, other, out):
    high = lax.div(lax.axis_index("layer"), 4)
    left_own = rows[:, 0].reshape(ROWS * HALF, WIDTH)
    left_other = rows[:, 1].reshape(ROWS * HALF, WIDTH)
    dims = (((1,), (1,)), ((), ()))
    for part in range(4):
        span = pl.ds(part * WIDTH, WIDTH)
        total = triple_dot(left_own, own[span, :], dims)
        total += triple_dot(left_other, other[span, :], dims)
        q, side = divmod(part, 2)
        for i in range(ROWS):
            out[2 * i + (q ^ high), :, side * WIDTH : (side + 1) * WIDTH] = total[
                i * HALF : (i + 1) * HALF
            ]


def second_kernel(square, own, other, out):
    high = lax.div(lax.axis_index("layer"), 4)
    core = lax.rem(lax.axis_index("col"), 2)
    dims = (((1,), (0,)), ((), ()))
    for side, panel in ((0, own), (1, other)):
        total = jnp.zeros((ROWS * HALF, WIDTH), jnp.float32)
        for part in range(4):
            q, half = divmod(part, 2)
            left = jnp.concatenate(
                [
                    square[2 * i + (q ^ high), :, half * WIDTH : (half + 1) * WIDTH]
                    for i in range(ROWS)
                ],
                axis=0,
            )
            total += triple_dot(left, panel[pl.ds(part * WIDTH, WIDTH), :], dims)
        for i in range(ROWS):
            out[i, lax.rem(core + side, 2)] = total[i * HALF : (i + 1) * HALF]


def finish_kernel(cube, first, second, square, purified):
    even = lax.rem(lax.axis_index("layer"), 2) == 0
    home = jnp.concatenate(
        [
            jnp.where(even, first[...], second[...]).T,
            jnp.where(even, second[...], first[...]).T,
        ],
        axis=1,
    )
    square[...] = home
    for c in range(2):
        rows = slice(c * HALF, (c + 1) * HALF)
        total = (cube[c] + cube[2 + c]) + (cube[4 + c] + cube[6 + c])
        purified[rows] = 3.0 * home[rows] - 2.0 * total


def mask_kernel(pattern, density, out, masked, sems):
    row = lax.axis_index("row") * LAYERS + lax.axis_index("layer")
    col = lax.axis_index("col")
    for h in range(2):
        kept = pattern[row, 2 * col + h].astype(jnp.float32)
        span = slice(h * BLK, (h + 1) * BLK)
        masked[:, span] = density[:, span] * kept
    sends = [pltpu.make_async_copy(masked, out.at[k], sems.at[k]) for k in range(LAYERS)]
    for send in sends:
        send.start()
    for send in sends:
        send.wait()


def masked_copies(pattern, density):
    return pl.pallas_call(
        mask_kernel,
        out_shape=(
            jax.ShapeDtypeStruct((LAYERS, BLK, WIDTH), jnp.float32),
            jax.ShapeDtypeStruct((BLK, WIDTH), jnp.float32),
        ),
        in_specs=[
            pl.BlockSpec(memory_space=pltpu.SMEM),
            pl.BlockSpec(memory_space=pltpu.VMEM),
        ],
        out_specs=(pl.BlockSpec(memory_space=pl.ANY), pl.BlockSpec(memory_space=pltpu.VMEM)),
        scratch_shapes=[pltpu.SemaphoreType.DMA((LAYERS,))],
        cost_estimate=pl.CostEstimate(
            flops=BLK * WIDTH, bytes_accessed=9 * BLK * WIDTH * 4, transcendentals=0
        ),
    )(pattern, density)


def call(kernel, shapes, *operands, flops=6 * 256 * 512 * 1024):
    return pl.pallas_call(
        kernel,
        out_shape=[jax.ShapeDtypeStruct(shape, jnp.float32) for shape in shapes],
        in_specs=[pl.BlockSpec(memory_space=pltpu.VMEM)] * len(operands),
        out_specs=[pl.BlockSpec(memory_space=pltpu.VMEM)] * len(shapes),
        compiler_params=pltpu.CompilerParams(vmem_limit_bytes=32 * 1024 * 1024),
        cost_estimate=pl.CostEstimate(
            flops=flops, bytes_accessed=1024 * 1024, transcendentals=0
        ),
    )(*operands)


def swap_core(value):
    return lax.ppermute(value, "col", [(i, i ^ 1) for i in range(16)])


def near_exchange(value):
    groups = [[chip * 2 + core for chip in range(NEAR)] for core in range(2)]
    return lax.all_to_all(value, "col", 0, 0, axis_index_groups=groups)


def copies(value, count):
    return jnp.broadcast_to(value[None], (count, *value.shape))


def mirror_home(piece, turn, layer):
    pairs = []
    for r in range(4):
        for c in range(16):
            for z in range(LAYERS):
                to = (r * 16 + c // 4 * 4 + z // 2) * LAYERS + (z ^ (2 * (c % 4) + turn))
                pairs.append(((r * 16 + c) * LAYERS + z, to))
    return lax.ppermute(piece[turn], ("row", "col", "layer"), pairs)


def whole_rows(piece, core, layer):
    blocks = [piece[:, k * BLK : (k + 1) * BLK] for k in range(4)]
    blocks = jnp.stack(blocks)
    pick = lambda c: jnp.stack(
        [
            lax.dynamic_index_in_dim(blocks, (layer % 4) ^ (2 * c + j), 0, keepdims=False)
            for j in range(2)
        ]
    )
    mine, theirs = pick(core), swap_core(pick(1 - core))
    return jnp.where(
        core == 0,
        jnp.concatenate([mine, theirs], axis=1),
        jnp.concatenate([theirs, mine], axis=1),
    )


def body(density, pattern):
    core = lax.axis_index("col") % 2
    sends, masked = masked_copies(pattern, density)

    own = lax.all_to_all(sends, "layer", 0, 0).reshape(LAYERS * BLK, WIDTH)

    halves = masked.reshape(2, HALF, WIDTH)
    mine = lax.dynamic_index_in_dim(halves, core, 0, keepdims=False)
    theirs = lax.dynamic_index_in_dim(halves, 1 - core, 0, keepdims=False)
    rows = jnp.concatenate([mine, swap_core(theirs)], axis=0)
    rows = lax.all_gather(rows, "row").reshape(ROWS, 2, HALF, WIDTH)

    own, rows = lax.optimization_barrier((own, rows))
    other = swap_core(own)
    (square_terms,) = call(first_kernel, [(NEAR, HALF, 2 * WIDTH)], rows, own, other)
    square_piece = jnp.sum(near_exchange(square_terms), axis=0)
    square_rows = near_exchange(copies(square_piece, NEAR))
    layer = lax.axis_index("layer")
    piece = whole_rows(square_piece, core, layer)
    square_rows, piece = lax.optimization_barrier((square_rows, piece))
    first, second = mirror_home(piece, 0, layer), mirror_home(piece, 1, layer)

    (cube_terms,) = call(second_kernel, [(ROWS, 2, HALF, WIDTH)], square_rows, own, other)
    homes = [
        [r * 16 + chip * 2 + c for r in range(ROWS) for c in range(2)] for chip in range(NEAR)
    ]
    cube_terms = cube_terms.reshape(ROWS * 2, HALF, WIDTH)
    cube = lax.all_to_all(cube_terms, ("row", "col"), 0, 0, axis_index_groups=homes)
    cube, first, second = lax.optimization_barrier((cube, first, second))
    square, purified = call(
        finish_kernel, [(BLK, WIDTH)] * 2, cube, first, second, flops=16 * BLK * WIDTH
    )
    return (square, purified)


def solution(mesh):
    in_specs = (P(("row", "layer"), "col"), P())
    out_specs = (P(("row", "layer"), "col"), P(("row", "layer"), "col"))
    return jax.shard_map(body, mesh=mesh, in_specs=in_specs, out_specs=out_specs, check_vma=False)
```

time: 121 us -> 116 us (0.959)
  the two profiles are of different devices: /device:TPU:107 before, /device:TPU:1 now
where the time goes in v4:
time: 116 us; the launch traced here: 114 us
  starting transfers between devices  36.4 us (31%)
  blocking collectives  35.8 us (31%)
  waiting for transfers between devices  33.6 us (29%)
  Pallas kernels  5.47 us (5%)
  local copies, waits for them, and re-layouts  1.96 us (2%)
    all_to_all x1, blocking collectives, near_exchange(): return lax.all_to_all(value, 'col', 0, 0, axis_index_groups=groups)  19.7 us
    all_gather x1, blocking collectives, body(): rows = lax.all_gather(rows, 'row').reshape(ROWS, 2, HALF, WIDTH)  16.2 us
    all_to_all x1, starting transfers between devices, body(): own = lax.all_to_all(sends, 'layer', 0, 0).reshape(LAYERS * BLK, WIDTH)  11 us
    all_to_all x1, waiting for transfers between devices, body(): own = lax.all_to_all(sends, 'layer', 0, 0).reshape(LAYERS * BLK, WIDTH)  9.21 us
    all_to_all x1, waiting for transfers between devices, near_exchange(): return lax.all_to_all(value, 'col', 0, 0, axis_index_groups=groups)  9.1 us
    ppermute x3, starting transfers between devices, swap_core(): return lax.ppermute(value, 'col', [(i, i ^ 1) for i in range(16)])  8.99 us
    all_to_all x1, starting transfers between devices, body(): lax.all_to_all(cube_terms, ('row', 'col'), 0, 0, axis_index_groups=homes)  8.95 us
    all_to_all x1, waiting for transfers between devices, body(): lax.all_to_all(cube_terms, ('row', 'col'), 0, 0, axis_index_groups=homes)  7.11 us
  transfers between devices with their start and end apart: 8, of which 8 were waited for; matrix products, arithmetic and copies ran while one was open for 0% of the time, Pallas kernels for 0%

profile of v4, /device:TPU:1, one launch (start us, length us, event | category | flops | bytes accessed | tf_op | source)
XLA Modules:
  0.0 114.3 jit_solution(10043365140336880398)
XLA Ops:
  0.6 2.7 %shard_map.41 = (f32[8,128,256]{2,1,0:T(8,128)}, f32[128,256]{1,0:T(8,128)}) custom-call(s32[32,32]{1,0:T(8,128)} %pattern.1, f32[128,256]{1,0:T(8,128)} %density.1), custom_call_target="tpu_custom_call" | custom-call | flops 32768 | bytes 1179648 | tf_op jit(solution)/shard_map/pallas_call | solution.py:96
  3.3 11.0 %all-to-all-start = ((f32[8,128,256]{2,1,0:T(8,128)}), f32[8,128,256]{2,1,0:T(8,128)S(1)}, u32[]{:S(2)}, u32[]{:S(2)}) async-start(f32[8,128,256]{2,1,0:T(8,128)} %get-tuple-element.11), calls=%async_computation | async-start | bytes 2097152 | tf_op jit(solution)/shard_map/all_to_all | solution.py:171
  14.3 2.9 %collective-permute-start = (f32[64,256]{1,0:T(8,128)S(1)}, f32[64,256]{1,0:T(8,128)S(1)}, u32[]{:S(2)}, u32[]{:S(2)}) collective-permute-start(f32[64,256]{1,0:T(8,128)S(1)} %get-tuple-element.31), channel_id=1, source_target_pairs={{0,8},{8,0},{16,24},{24,16},{32,40},{40,32},{48,56},{56,48},{64,72... | collective-permute-start | bytes 196616 | tf_op jit(solution)/shard_map/ppermute | solution.py:128
  17.2 0.9 collective-permute-done
  18.1 16.2 %all-gather = f32[512,256]{1,0:T(8,128)S(1)} all-gather(f32[128,256]{1,0:T(8,128)S(1)} %pad_maximum_fusion), channel_id=2, replica_groups=mesh['row'=4,'col'=16,'layer'=8] {'row'}, dimensions={0}, use_global_device_ids=true | all-gather | bytes 655360 | tf_op jit(solution)/shard_map/all_gather | solution.py:177
  34.3 9.2 %all-to-all-done = f32[8,128,256]{2,1,0:T(8,128)S(1)} async-done(((f32[8,128,256]{2,1,0:T(8,128)}), f32[8,128,256]{2,1,0:T(8,128)S(1)}, u32[]{:S(2)}, u32[]{:S(2)}) %all-to-all-start) | async-done | bytes 1048608 | tf_op jit(solution)/shard_map/all_to_all | solution.py:171
  43.5 2.4 %collective-permute-start.1 = (f32[1024,256]{1,0:T(8,128)S(1)}, f32[1024,256]{1,0:T(8,128)S(1)}, u32[]{:S(2)}, u32[]{:S(2)}) collective-permute-start(f32[1024,256]{1,0:T(8,128)S(1)} %bitcast.20), channel_id=1, source_target_pairs={{0,8},{8,0},{16,24},{24,16},{32,40},{40,32},{48,56},{56,48},{64,72... | collective-permute-start | bytes 3145736 | tf_op jit(solution)/shard_map/ppermute | solution.py:128
  45.9 2.3 %collective-permute-done.1.other = f32[1024,256]{1,0:T(8,128)S(1)} collective-permute-done((f32[1024,256]{1,0:T(8,128)S(1)}, f32[1024,256]{1,0:T(8,128)S(1)}, u32[]{:S(2)}, u32[]{:S(2)}) %collective-permute-start.1) | collective-permute-done | bytes 1048608 | tf_op jit(solution)/shard_map/ppermute | solution.py:128
  48.2 1.0 shard_map.42
  49.2 19.7 %all_to_all.20 = f32[8,64,512]{2,1,0:T(8,128)S(1)} all-to-all(f32[8,64,512]{2,1,0:T(8,128)S(1)} %shard_map.42), channel_id=1, replica_groups={{0,16,32,48,64,80,96,112},{8,24,40,56,72,88,104,120},{1,17,33,49,65,81,..., dimensions={0} | all-to-all | bytes 2097152 | tf_op jit(solution)/shard_map/all_to_all | solution.py:133
  68.9 1.1 broadcast_in_dim.2
  70.0 3.6 %all-to-all-start.2 = ((f32[8,64,512]{2,1,0:T(8,128)}), f32[8,64,512]{2,1,0:T(8,128)S(1)}, u32[]{:S(2)}, u32[]{:S(2)}) async-start(f32[8,64,512]{2,1,0:T(8,128)} %broadcast_in_dim.2), calls=%async_computation.2 | async-start | bytes 2097152 | tf_op jit(solution)/shard_map/all_to_all | solution.py:133
  73.7 3.7 %collective-permute-start.2 = (f32[2,64,128]{2,1,0:T(8,128)S(1)}, f32[2,64,128]{2,1,0:T(8,128)S(1)}, u32[]{:S(2)}, u32[]{:S(2)}) collective-permute-start(f32[2,64,128]{2,1,0:T(8,128)S(1)} %pad_maximum_fusion.2), channel_id=1, source_target_pairs={{0,8},{8,0},{16,24},{24,16},{32,40},{40,32},{48,56},{56,48},{64,72... | collective-permute-start | bytes 196616 | tf_op jit(solution)/shard_map/ppermute | solution.py:128
  77.5 0.9 collective-permute-done.2
  78.4 9.1 %all-to-all-done.2.square = f32[8,64,512]{2,1,0:T(8,128)S(1)} async-done(((f32[8,64,512]{2,1,0:T(8,128)}), f32[8,64,512]{2,1,0:T(8,128)S(1)}, u32[]{:S(2)}, u32[]{:S(2)}) %all-to-all-start.2) | async-done | bytes 1048608 | tf_op jit(solution)/shard_map/all_to_all | solution.py:133
  87.5 1.0 shard_map.43
  88.5 0.8 copy-done
  89.3 9.0 %all-to-all-start.3 = ((f32[8,64,256]{2,1,0:T(8,128)}), f32[8,64,256]{2,1,0:T(8,128)S(1)}, u32[]{:S(2)}, u32[]{:S(2)}) async-start(f32[8,64,256]{2,1,0:T(8,128)} %bitcast.24), calls=%async_computation.3 | async-start | bytes 1048576 | tf_op jit(solution)/shard_map/all_to_all | solution.py:194
  98.2 1.9 %collective-permute-start.4 = (f32[128,128]{1,0:T(8,128)S(1)}, f32[128,128]{1,0:T(8,128)S(1)}, u32[]{:S(2)}, u32[]{:S(2)}) collective-permute-start(f32[128,128]{1,0:T(8,128)S(1)} %get-tuple-element.20), channel_id=1, source_target_pairs={{0,1},{1,0},{2,11},{3,10},{4,21},{5,20},{6,31},{7,30},{8,3},{9,2},... | collective-permute-start | bytes 196616 | tf_op jit(solution)/shard_map/ppermute | solution.py:147
  100.2 2.0 %collective-permute-start.3 = (f32[128,128]{1,0:T(8,128)S(1)}, f32[128,128]{1,0:T(8,128)S(1)}, u32[]{:S(2)}, u32[]{:S(2)}) collective-permute-start(f32[128,128]{1,0:T(8,128)S(1)} %get-tuple-element.21), channel_id=1, source_target_pairs={{0,0},{1,1},{2,10},{3,11},{4,20},{5,21},{6,30},{7,31},{8,2},{9,3},... | collective-permute-start | bytes 196616 | tf_op jit(solution)/shard_map/ppermute | solution.py:147
  102.2 3.2 %collective-permute-done.4.second = f32[128,128]{1,0:T(8,128)S(1)} collective-permute-done((f32[128,128]{1,0:T(8,128)S(1)}, f32[128,128]{1,0:T(8,128)S(1)}, u32[]{:S(2)}, u32[]{:S(2)}) %collective-permute-start.4) | collective-permute-done | bytes 65568 | tf_op jit(solution)/shard_map/ppermute | solution.py:147
  105.3 1.0 collective-permute-done.3.first
  106.4 7.1 %all-to-all-done.3.cube = f32[8,64,256]{2,1,0:T(8,128)S(1)} async-done(((f32[8,64,256]{2,1,0:T(8,128)}), f32[8,64,256]{2,1,0:T(8,128)S(1)}, u32[]{:S(2)}, u32[]{:S(2)}) %all-to-all-start.3) | async-done | bytes 524320 | tf_op jit(solution)/shard_map/all_to_all | solution.py:194
  113.5 0.8 shard_map.44
  (12 shorter events, 0.2 us)
Async XLA Ops:
  3.3 11.0 %copy-start.1 = (f32[128,256]{1,0:T(8,128)S(1)}, f32[128,256]{1,0:T(8,128)}, u32[]{:S(2)}) copy-start(f32[128,256]{1,0:T(8,128)} %get-tuple-element.12) | copy-start | bytes 393220
  3.3 40.2 %all-to-all-start = ((f32[8,128,256]{2,1,0:T(8,128)}), f32[8,128,256]{2,1,0:T(8,128)S(1)}, u32[]{:S(2)}, u32[]{:S(2)}) async-start(f32[8,128,256]{2,1,0:T(8,128)} %get-tuple-element.11), calls=%async_computation | async-start | bytes 2097152 | tf_op jit(solution)/shard_map/all_to_all | solution.py:171
  14.3 3.8 %collective-permute-start = (f32[64,256]{1,0:T(8,128)S(1)}, f32[64,256]{1,0:T(8,128)S(1)}, u32[]{:S(2)}, u32[]{:S(2)}) collective-permute-start(f32[64,256]{1,0:T(8,128)S(1)} %get-tuple-element.31), channel_id=1, source_target_pairs={{0,8},{8,0},{16,24},{24,16},{32,40},{40,32},{48,56},{56,48},{64,72... | collective-permute-start | bytes 196616 | tf_op jit(solution)/shard_map/ppermute | solution.py:128
  43.5 4.7 %collective-permute-start.1 = (f32[1024,256]{1,0:T(8,128)S(1)}, f32[1024,256]{1,0:T(8,128)S(1)}, u32[]{:S(2)}, u32[]{:S(2)}) collective-permute-start(f32[1024,256]{1,0:T(8,128)S(1)} %bitcast.20), channel_id=1, source_target_pairs={{0,8},{8,0},{16,24},{24,16},{32,40},{40,32},{48,56},{56,48},{64,72... | collective-permute-start | bytes 3145736 | tf_op jit(solution)/shard_map/ppermute | solution.py:128
  70.0 17.4 %all-to-all-start.2 = ((f32[8,64,512]{2,1,0:T(8,128)}), f32[8,64,512]{2,1,0:T(8,128)S(1)}, u32[]{:S(2)}, u32[]{:S(2)}) async-start(f32[8,64,512]{2,1,0:T(8,128)} %broadcast_in_dim.2), calls=%async_computation.2 | async-start | bytes 2097152 | tf_op jit(solution)/shard_map/all_to_all | solution.py:133
  73.7 4.6 %collective-permute-start.2 = (f32[2,64,128]{2,1,0:T(8,128)S(1)}, f32[2,64,128]{2,1,0:T(8,128)S(1)}, u32[]{:S(2)}, u32[]{:S(2)}) collective-permute-start(f32[2,64,128]{2,1,0:T(8,128)S(1)} %pad_maximum_fusion.2), channel_id=1, source_target_pairs={{0,8},{8,0},{16,24},{24,16},{32,40},{40,32},{48,56},{56,48},{64,72... | collective-permute-start | bytes 196616 | tf_op jit(solution)/shard_map/ppermute | solution.py:128
  88.5 0.8 copy-start
  89.3 24.2 %all-to-all-start.3 = ((f32[8,64,256]{2,1,0:T(8,128)}), f32[8,64,256]{2,1,0:T(8,128)S(1)}, u32[]{:S(2)}, u32[]{:S(2)}) async-start(f32[8,64,256]{2,1,0:T(8,128)} %bitcast.24), calls=%async_computation.3 | async-start | bytes 1048576 | tf_op jit(solution)/shard_map/all_to_all | solution.py:194
  98.2 7.1 %collective-permute-start.4 = (f32[128,128]{1,0:T(8,128)S(1)}, f32[128,128]{1,0:T(8,128)S(1)}, u32[]{:S(2)}, u32[]{:S(2)}) collective-permute-start(f32[128,128]{1,0:T(8,128)S(1)} %get-tuple-element.20), channel_id=1, source_target_pairs={{0,1},{1,0},{2,11},{3,10},{4,21},{5,20},{6,31},{7,30},{8,3},{9,2},... | collective-permute-start | bytes 196616 | tf_op jit(solution)/shard_map/ppermute | solution.py:147
  100.2 6.2 %collective-permute-start.3 = (f32[128,128]{1,0:T(8,128)S(1)}, f32[128,128]{1,0:T(8,128)S(1)}, u32[]{:S(2)}, u32[]{:S(2)}) collective-permute-start(f32[128,128]{1,0:T(8,128)S(1)} %get-tuple-element.21), channel_id=1, source_target_pairs={{0,0},{1,1},{2,10},{3,11},{4,20},{5,21},{6,30},{7,31},{8,2},{9,3},... | collective-permute-start | bytes 196616 | tf_op jit(solution)/shard_map/ppermute | solution.py:147

commit v5 on v4

v5 whole, which is shorter than its diff:
```python
import jax
import jax.numpy as jnp
from jax import lax
from jax.experimental import pallas as pl
from jax.experimental.pallas import tpu as pltpu
from jax.sharding import PartitionSpec as P

BLK = 128
HALF = 64
WIDTH = 256
ROWS = 4
NEAR = 8
LAYERS = 8


def split(value):
    high = value.astype(jnp.bfloat16)
    return high, (value - high.astype(jnp.float32)).astype(jnp.bfloat16)


def triple_dot(left, right, dims):
    left_high, left_low = split(left)
    right_high, right_low = split(right)
    total = lax.dot_general(left_high, right_low, dims, preferred_element_type=jnp.float32)
    total += lax.dot_general(left_low, right_high, dims, preferred_element_type=jnp.float32)
    return total + lax.dot_general(left_high, right_high, dims, preferred_element_type=jnp.float32)


def first_kernel(rows, own, other, rows_kept, panel_kept, out):
    high = lax.div(lax.axis_index("layer"), 4)
    lefts = [
        jnp.concatenate(
            [rows[i, side] * rows_kept[side, i : i + 1, :] for i in range(ROWS)], axis=0
        )
        for side in range(2)
    ]
    dims = (((1,), (1,)), ((), ()))
    for part in range(4):
        total = triple_dot(lefts[0], panel_part(own, panel_kept, 0, part), dims)
        total += triple_dot(lefts[1], panel_part(other, panel_kept, 1, part), dims)
        q, half = divmod(part, 2)
        for i in range(ROWS):
            out[2 * i + (q ^ high), :, half * WIDTH : (half + 1) * WIDTH] = total[
                i * HALF : (i + 1) * HALF
            ]


def panel_part(panel, kept, side, part):
    return jnp.concatenate(
        [panel[z * BLK : (z + 1) * BLK, :] * kept[side, z : z + 1, :] for z in (2 * part, 2 * part + 1)],
        axis=0,
    )


def second_kernel(square, own, other, panel_kept, out):
    high = lax.div(lax.axis_index("layer"), 4)
    core = lax.rem(lax.axis_index("col"), 2)
    dims = (((1,), (0,)), ((), ()))
    for side, panel in ((0, own), (1, other)):
        total = jnp.zeros((ROWS * HALF, WIDTH), jnp.float32)
        for part in range(4):
            q, half = divmod(part, 2)
            left = jnp.concatenate(
                [
                    square[2 * i + (q ^ high), :, half * WIDTH : (half + 1) * WIDTH]
                    for i in range(ROWS)
                ],
                axis=0,
            )
            total += triple_dot(left, panel_part(panel, panel_kept, side, part), dims)
        for i in range(ROWS):
            out[i, lax.rem(core + side, 2)] = total[i * HALF : (i + 1) * HALF]


def finish_kernel(cube, mirrored, square, purified):
    home = mirrored[...].T
    square[...] = home
    for c in range(2):
        rows = slice(c * HALF, (c + 1) * HALF)
        total = (cube[c] + cube[2 + c]) + (cube[4 + c] + cube[6 + c])
        purified[rows] = 3.0 * home[rows] - 2.0 * total


def call(kernel, shapes, *operands, flops):
    return pl.pallas_call(
        kernel,
        out_shape=[jax.ShapeDtypeStruct(shape, jnp.float32) for shape in shapes],
        in_specs=[pl.BlockSpec(memory_space=pltpu.VMEM)] * len(operands),
        out_specs=[pl.BlockSpec(memory_space=pltpu.VMEM)] * len(shapes),
        compiler_params=pltpu.CompilerParams(vmem_limit_bytes=32 * 1024 * 1024),
        cost_estimate=pl.CostEstimate(
            flops=flops, bytes_accessed=1024 * 1024, transcendentals=0
        ),
    )(*operands)


def kept_columns(pattern, col):
    both = [lax.dynamic_slice_in_dim(pattern, 2 * (col ^ side), 2, axis=1) for side in range(2)]
    return jnp.repeat(jnp.stack(both).astype(jnp.float32), BLK, axis=2)


def swap_core(value):
    return lax.ppermute(value, "col", [(i, i ^ 1) for i in range(16)])


def near_exchange(value):
    groups = [[chip * 2 + core for chip in range(NEAR)] for core in range(2)]
    return lax.all_to_all(value, "col", 0, 0, axis_index_groups=groups)


def copies(value, count):
    return jnp.broadcast_to(value[None], (count, *value.shape))


def mirror_home(piece):
    pairs = []
    for r in range(4):
        for c in range(16):
            for z in range(LAYERS):
                to = (r * 16 + c // 4 * 4 + z // 2) * LAYERS + (z ^ (2 * (c % 4)))
                pairs.append(((r * 16 + c) * LAYERS + z, to))
    return lax.ppermute(piece, ("row", "col", "layer"), pairs)


def layer_pair(pieces, layer):
    received = lax.ppermute(pieces[1], "layer", [(z, z ^ 1) for z in range(LAYERS)])
    return jnp.where(
        layer % 2 == 0,
        jnp.concatenate([pieces[0], received], axis=0),
        jnp.concatenate([received, pieces[0]], axis=0),
    )


def whole_rows(piece, core, layer):
    blocks = [piece[:, k * BLK : (k + 1) * BLK] for k in range(4)]
    blocks = jnp.stack(blocks)
    pick = lambda c: jnp.stack(
        [
            lax.dynamic_index_in_dim(blocks, (layer % 4) ^ (2 * c + j), 0, keepdims=False)
            for j in range(2)
        ]
    )
    mine, theirs = pick(core), swap_core(pick(1 - core))
    return jnp.where(
        core == 0,
        jnp.concatenate([mine, theirs], axis=1),
        jnp.concatenate([theirs, mine], axis=1),
    )


def body(density, pattern):
    row, col, layer = (lax.axis_index(name) for name in ("row", "col", "layer"))
    core = col % 2
    row_groups = pattern.reshape(ROWS, LAYERS, ROWS * LAYERS)
    panel_kept = kept_columns(lax.dynamic_index_in_dim(row_groups, row, 0, keepdims=False), col)
    rows_kept = kept_columns(lax.dynamic_index_in_dim(row_groups, layer, 1, keepdims=False), col)

    own = lax.all_to_all(copies(density, LAYERS), "layer", 0, 0).reshape(LAYERS * BLK, WIDTH)

    halves = density.reshape(2, HALF, WIDTH)
    mine = lax.dynamic_index_in_dim(halves, core, 0, keepdims=False)
    theirs = lax.dynamic_index_in_dim(halves, 1 - core, 0, keepdims=False)
    rows = jnp.concatenate([mine, swap_core(theirs)], axis=0)
    rows = lax.all_gather(rows, "row").reshape(ROWS, 2, HALF, WIDTH)

    own, rows = lax.optimization_barrier((own, rows))
    other = swap_core(own)
    flops = 6 * 256 * 512 * 1024
    (square_terms,) = call(
        first_kernel,
        [(NEAR, HALF, 2 * WIDTH)],
        rows,
        own,
        other,
        rows_kept,
        panel_kept,
        flops=flops,
    )
    square_piece = jnp.sum(near_exchange(square_terms), axis=0)
    square_rows = near_exchange(copies(square_piece, NEAR))
    piece = layer_pair(whole_rows(square_piece, core, layer), layer)
    square_rows, piece = lax.optimization_barrier((square_rows, piece))
    mirrored = mirror_home(piece)

    (cube_terms,) = call(
        second_kernel,
        [(ROWS, 2, HALF, WIDTH)],
        square_rows,
        own,
        other,
        panel_kept,
        flops=flops,
    )
    homes = [
        [r * 16 + chip * 2 + c for r in range(ROWS) for c in range(2)] for chip in range(NEAR)
    ]
    cube_terms = cube_terms.reshape(ROWS * 2, HALF, WIDTH)
    cube = lax.all_to_all(cube_terms, ("row", "col"), 0, 0, axis_index_groups=homes)
    cube, mirrored = lax.optimization_barrier((cube, mirrored))
    square, purified = call(
        finish_kernel, [(BLK, WIDTH)] * 2, cube, mirrored, flops=16 * BLK * WIDTH
    )
    return (square, purified)


def solution(mesh):
    in_specs = (P(("row", "layer"), "col"), P())
    out_specs = (P(("row", "layer"), "col"), P(("row", "layer"), "col"))
    return jax.shard_map(body, mesh=mesh, in_specs=in_specs, out_specs=out_specs, check_vma=False)
```

time: 116 us -> 115 us (level)
  local copies, waits for them, and re-layouts: 1.96 us -> 5.42 us
  Pallas kernels: 5.47 us -> 2.82 us
  waiting for transfers between devices: 33.6 us -> 31.8 us
    all_to_all x1, waiting for transfers between devices: 9.1 us -> 3.76 us  [near_exchange(): return lax.all_to_all(value, 'col', 0, 0, axis_index_groups=groups)]
    ppermute x2, waiting for transfers between devices: 4.2 us -> 9.38 us  [the longest x1 6.3 us: mirror_home(): return lax.ppermute(piece, ('row', 'col', 'layer'), pairs)]
    pallas_call x1 -> x0, Pallas kernels: 2.66 us -> none  [masked_copies(): pl.pallas_call(mask_kernel, out_shape=(jax.ShapeDtypeStruct((LAYERS, BLK,...]
    broadcast_in_dim x1 -> x2, local copies, waits for them, and re-layouts: 1.11 us -> 3.09 us  [copies(): return jnp.broadcast_to(value[None], (count, *value.shape))]
    ppermute x3, waiting for transfers between devices: 4.02 us -> 2.49 us  [swap_core(): return lax.ppermute(value, 'col', [(i, i ^ 1) for i in range(16)])]
  transfers between devices with their start and end apart: 8 -> 8, of which waited for: 8 -> 8; matrix products, arithmetic and copies ran while one was open for 0% -> 1% of each run, Pallas kernels for 0% -> 0%
where the time goes in v5:
time: 115 us; the launch traced here: 114 us
  starting transfers between devices  36.7 us (32%)
  blocking collectives  35.8 us (31%)
  waiting for transfers between devices  31.8 us (28%)
  local copies, waits for them, and re-layouts  5.42 us (5%)
  Pallas kernels  2.82 us (2%)
    all_to_all x1, blocking collectives, near_exchange(): return lax.all_to_all(value, 'col', 0, 0, axis_index_groups=groups)  19.6 us
    all_gather x1, blocking collectives, body(): rows = lax.all_gather(rows, 'row').reshape(ROWS, 2, HALF, WIDTH)  16.2 us
    all_to_all x1, starting transfers between devices, body(): lax.all_to_all(copies(density, LAYERS), 'layer', 0, 0)  11 us
    all_to_all x1, waiting for transfers between devices, body(): lax.all_to_all(copies(density, LAYERS), 'layer', 0, 0)  9.21 us
    ppermute x3, starting transfers between devices, swap_core(): return lax.ppermute(value, 'col', [(i, i ^ 1) for i in range(16)])  8.99 us
    all_to_all x1, starting transfers between devices, body(): lax.all_to_all(cube_terms, ('row', 'col'), 0, 0, axis_index_groups=homes)  8.95 us
    all_to_all x1, waiting for transfers between devices, body(): lax.all_to_all(cube_terms, ('row', 'col'), 0, 0, axis_index_groups=homes)  6.96 us
    ppermute x1, waiting for transfers between devices, mirror_home(): return lax.ppermute(piece, ('row', 'col', 'layer'), pairs)  6.3 us
  transfers between devices with their start and end apart: 8, of which 8 were waited for; matrix products, arithmetic and copies ran while one was open for 1% of the time, Pallas kernels for 0%

profile of v5, /device:TPU:1, one launch (start us, length us, event | category | flops | bytes accessed | tf_op | source)
XLA Modules:
  0.0 113.6 jit_solution(6640851387117893973)
XLA Ops:
  0.6 2.0 %broadcast_in_dim.8 = f32[8,128,256]{2,1,0:T(8,128)} broadcast(f32[128,256]{1,0:T(8,128)} %param.2), dimensions={1,2} | broadcast | bytes 1179648 | tf_op jit(solution)/shard_map/broadcast_in_dim | solution.py:112
  2.6 11.0 %all-to-all-start = ((f32[8,128,256]{2,1,0:T(8,128)}), f32[8,128,256]{2,1,0:T(8,128)S(1)}, u32[]{:S(2)}, u32[]{:S(2)}) async-start(f32[8,128,256]{2,1,0:T(8,128)} %broadcast_in_dim.8), calls=%async_computation | async-start | bytes 2097152 | tf_op jit(solution)/shard_map/all_to_all | solution.py:158
  13.6 2.9 %collective-permute-start = (f32[64,256]{1,0:T(8,128)S(1)}, f32[64,256]{1,0:T(8,128)S(1)}, u32[]{:S(2)}, u32[]{:S(2)}) collective-permute-start(f32[64,256]{1,0:T(8,128)S(1)} %get-tuple-element.25), channel_id=1, source_target_pairs={{0,8},{8,0},{16,24},{24,16},{32,40},{40,32},{48,56},{56,48},{64,72... | collective-permute-start | bytes 196616 | tf_op jit(solution)/shard_map/ppermute | solution.py:103
  16.5 0.9 collective-permute-done
  17.4 16.2 %all-gather = f32[512,256]{1,0:T(8,128)S(1)} all-gather(f32[128,256]{1,0:T(8,128)S(1)} %pad_maximum_fusion), channel_id=2, replica_groups=mesh['row'=4,'col'=16,'layer'=8] {'row'}, dimensions={0}, use_global_device_ids=true | all-gather | bytes 655360 | tf_op jit(solution)/shard_map/all_gather | solution.py:164
  33.6 9.2 %all-to-all-done = f32[8,128,256]{2,1,0:T(8,128)S(1)} async-done(((f32[8,128,256]{2,1,0:T(8,128)}), f32[8,128,256]{2,1,0:T(8,128)S(1)}, u32[]{:S(2)}, u32[]{:S(2)}) %all-to-all-start) | async-done | bytes 1048608 | tf_op jit(solution)/shard_map/all_to_all | solution.py:158
  42.8 2.4 %collective-permute-start.1 = (f32[1024,256]{1,0:T(8,128)S(1)}, f32[1024,256]{1,0:T(8,128)S(1)}, u32[]{:S(2)}, u32[]{:S(2)}) collective-permute-start(f32[1024,256]{1,0:T(8,128)S(1)} %bitcast.25), channel_id=1, source_target_pairs={{0,8},{8,0},{16,24},{24,16},{32,40},{40,32},{48,56},{56,48},{64,72... | collective-permute-start | bytes 3145736 | tf_op jit(solution)/shard_map/ppermute | solution.py:103
  46.7 0.7 collective-permute-done.1.other
  47.5 1.0 shard_map.41
  48.5 19.6 %all_to_all.20 = f32[8,64,512]{2,1,0:T(8,128)S(1)} all-to-all(f32[8,64,512]{2,1,0:T(8,128)S(1)} %shard_map.41), channel_id=1, replica_groups={{0,16,32,48,64,80,96,112},{8,24,40,56,72,88,104,120},{1,17,33,49,65,81,..., dimensions={0} | all-to-all | bytes 2097152 | tf_op jit(solution)/shard_map/all_to_all | solution.py:108
  68.2 1.1 broadcast_in_dim.21
  69.3 3.6 %all-to-all-start.2 = ((f32[8,64,512]{2,1,0:T(8,128)}), f32[8,64,512]{2,1,0:T(8,128)S(1)}, u32[]{:S(2)}, u32[]{:S(2)}) async-start(f32[8,64,512]{2,1,0:T(8,128)} %broadcast_in_dim.21), calls=%async_computation.2 | async-start | bytes 2097152 | tf_op jit(solution)/shard_map/all_to_all | solution.py:108
  73.0 3.7 %collective-permute-start.2 = (f32[2,64,128]{2,1,0:T(8,128)S(1)}, f32[2,64,128]{2,1,0:T(8,128)S(1)}, u32[]{:S(2)}, u32[]{:S(2)}) collective-permute-start(f32[2,64,128]{2,1,0:T(8,128)S(1)} %pad_maximum_fusion.2), channel_id=1, source_target_pairs={{0,8},{8,0},{16,24},{24,16},{32,40},{40,32},{48,56},{56,48},{64,72... | collective-permute-start | bytes 196616 | tf_op jit(solution)/shard_map/ppermute | solution.py:103
  76.8 0.9 collective-permute-done.2
  77.7 2.2 %collective-permute-start.3 = (f32[128,128]{1,0:T(8,128)S(1)}, f32[128,128]{1,0:T(8,128)S(1)}, u32[]{:S(2)}, u32[]{:S(2)}) collective-permute-start(f32[128,128]{1,0:T(8,128)S(1)} %get-tuple-element.15), channel_id=1, source_target_pairs={{0,1},{1,0},{2,3},{3,2},{4,5},{5,4},{6,7},{7,6},{8,9},{9,8},{10,11... | collective-permute-start | bytes 196616 | tf_op jit(solution)/shard_map/ppermute | solution.py:126
  79.9 3.1 %collective-permute-done.3 = f32[128,128]{1,0:T(8,128)S(1)} collective-permute-done((f32[128,128]{1,0:T(8,128)S(1)}, f32[128,128]{1,0:T(8,128)S(1)}, u32[]{:S(2)}, u32[]{:S(2)}) %collective-permute-start.3) | collective-permute-done | bytes 65568 | tf_op jit(solution)/shard_map/ppermute | solution.py:126
  83.0 3.8 %all-to-all-done.2.square = f32[8,64,512]{2,1,0:T(8,128)S(1)} async-done(((f32[8,64,512]{2,1,0:T(8,128)}), f32[8,64,512]{2,1,0:T(8,128)S(1)}, u32[]{:S(2)}, u32[]{:S(2)}) %all-to-all-start.2) | async-done | bytes 1048608 | tf_op jit(solution)/shard_map/all_to_all | solution.py:108
  86.8 1.0 shard_map.42
  87.8 0.8 copy-done
  88.6 9.0 %all-to-all-start.3 = ((f32[8,64,256]{2,1,0:T(8,128)}), f32[8,64,256]{2,1,0:T(8,128)S(1)}, u32[]{:S(2)}, u32[]{:S(2)}) async-start(f32[8,64,256]{2,1,0:T(8,128)} %bitcast.29), calls=%async_computation.3 | async-start | bytes 1048576 | tf_op jit(solution)/shard_map/all_to_all | solution.py:198
  97.5 2.0 %collective-permute-start.4 = (f32[256,128]{1,0:T(8,128)S(1)}, f32[256,128]{1,0:T(8,128)S(1)}, u32[]{:S(2)}, u32[]{:S(2)}) collective-permute-start(f32[256,128]{1,0:T(8,128)S(1)} %maximum_select_fusion.1), channel_id=1, source_target_pairs={{0,0},{1,1},{2,10},{3,11},{4,20},{5,21},{6,30},{7,31},{8,2},{9,3},... | collective-permute-start | bytes 393224 | tf_op jit(solution)/shard_map/ppermute | solution.py:122
  99.5 6.3 %collective-permute-done.4.mirrored = f32[256,128]{1,0:T(8,128)S(1)} collective-permute-done((f32[256,128]{1,0:T(8,128)S(1)}, f32[256,128]{1,0:T(8,128)S(1)}, u32[]{:S(2)}, u32[]{:S(2)}) %collective-permute-start.4) | collective-permute-done | bytes 131104 | tf_op jit(solution)/shard_map/ppermute | solution.py:122
  105.8 7.0 %all-to-all-done.3.cube = f32[8,64,256]{2,1,0:T(8,128)S(1)} async-done(((f32[8,64,256]{2,1,0:T(8,128)}), f32[8,64,256]{2,1,0:T(8,128)S(1)}, u32[]{:S(2)}, u32[]{:S(2)}) %all-to-all-start.3) | async-done | bytes 524320 | tf_op jit(solution)/shard_map/all_to_all | solution.py:198
  112.8 0.8 shard_map.43
  (27 shorter events, 1.7 us)
Async XLA Ops:
  2.6 11.0 %copy-start.1 = (f32[128,256]{1,0:T(8,128)S(1)}, f32[128,256]{1,0:T(8,128)}, u32[]{:S(2)}) copy-start(f32[128,256]{1,0:T(8,128)} %param.2) | copy-start | bytes 393220
  2.6 40.2 %all-to-all-start = ((f32[8,128,256]{2,1,0:T(8,128)}), f32[8,128,256]{2,1,0:T(8,128)S(1)}, u32[]{:S(2)}, u32[]{:S(2)}) async-start(f32[8,128,256]{2,1,0:T(8,128)} %broadcast_in_dim.8), calls=%async_computation | async-start | bytes 2097152 | tf_op jit(solution)/shard_map/all_to_all | solution.py:158
  13.6 3.8 %collective-permute-start = (f32[64,256]{1,0:T(8,128)S(1)}, f32[64,256]{1,0:T(8,128)S(1)}, u32[]{:S(2)}, u32[]{:S(2)}) collective-permute-start(f32[64,256]{1,0:T(8,128)S(1)} %get-tuple-element.25), channel_id=1, source_target_pairs={{0,8},{8,0},{16,24},{24,16},{32,40},{40,32},{48,56},{56,48},{64,72... | collective-permute-start | bytes 196616 | tf_op jit(solution)/shard_map/ppermute | solution.py:103
  42.8 4.7 %collective-permute-start.1 = (f32[1024,256]{1,0:T(8,128)S(1)}, f32[1024,256]{1,0:T(8,128)S(1)}, u32[]{:S(2)}, u32[]{:S(2)}) collective-permute-start(f32[1024,256]{1,0:T(8,128)S(1)} %bitcast.25), channel_id=1, source_target_pairs={{0,8},{8,0},{16,24},{24,16},{32,40},{40,32},{48,56},{56,48},{64,72... | collective-permute-start | bytes 3145736 | tf_op jit(solution)/shard_map/ppermute | solution.py:103
  45.2 0.7 copy-start.2
  69.3 17.4 %all-to-all-start.2 = ((f32[8,64,512]{2,1,0:T(8,128)}), f32[8,64,512]{2,1,0:T(8,128)S(1)}, u32[]{:S(2)}, u32[]{:S(2)}) async-start(f32[8,64,512]{2,1,0:T(8,128)} %broadcast_in_dim.21), calls=%async_computation.2 | async-start | bytes 2097152 | tf_op jit(solution)/shard_map/all_to_all | solution.py:108
  73.0 4.6 %collective-permute-start.2 = (f32[2,64,128]{2,1,0:T(8,128)S(1)}, f32[2,64,128]{2,1,0:T(8,128)S(1)}, u32[]{:S(2)}, u32[]{:S(2)}) collective-permute-start(f32[2,64,128]{2,1,0:T(8,128)S(1)} %pad_maximum_fusion.2), channel_id=1, source_target_pairs={{0,8},{8,0},{16,24},{24,16},{32,40},{40,32},{48,56},{56,48},{64,72... | collective-permute-start | bytes 196616 | tf_op jit(solution)/shard_map/ppermute | solution.py:103
  77.7 5.3 %collective-permute-start.3 = (f32[128,128]{1,0:T(8,128)S(1)}, f32[128,128]{1,0:T(8,128)S(1)}, u32[]{:S(2)}, u32[]{:S(2)}) collective-permute-start(f32[128,128]{1,0:T(8,128)S(1)} %get-tuple-element.15), channel_id=1, source_target_pairs={{0,1},{1,0},{2,3},{3,2},{4,5},{5,4},{6,7},{7,6},{8,9},{9,8},{10,11... | collective-permute-start | bytes 196616 | tf_op jit(solution)/shard_map/ppermute | solution.py:126
  87.8 0.8 copy-start
  88.6 24.2 %all-to-all-start.3 = ((f32[8,64,256]{2,1,0:T(8,128)}), f32[8,64,256]{2,1,0:T(8,128)S(1)}, u32[]{:S(2)}, u32[]{:S(2)}) async-start(f32[8,64,256]{2,1,0:T(8,128)} %bitcast.29), calls=%async_computation.3 | async-start | bytes 1048576 | tf_op jit(solution)/shard_map/all_to_all | solution.py:198
  97.5 8.3 %collective-permute-start.4 = (f32[256,128]{1,0:T(8,128)S(1)}, f32[256,128]{1,0:T(8,128)S(1)}, u32[]{:S(2)}, u32[]{:S(2)}) collective-permute-start(f32[256,128]{1,0:T(8,128)S(1)} %maximum_select_fusion.1), channel_id=1, source_target_pairs={{0,0},{1,1},{2,10},{3,11},{4,20},{5,21},{6,30},{7,31},{8,2},{9,3},... | collective-permute-start | bytes 393224 | tf_op jit(solution)/shard_map/ppermute | solution.py:122

commit v6 on v5

--- a/solution.py
+++ b/solution.py
@@ -28,6 +28,7 @@
 
 def first_kernel(rows, own, other, rows_kept, panel_kept, out):
     high = lax.div(lax.axis_index("layer"), 4)
+    turn = 4 * lax.rem(lax.axis_index("col"), 2)
     lefts = [
         jnp.concatenate(
             [rows[i, side] * rows_kept[side, i : i + 1, :] for i in range(ROWS)], axis=0
@@ -40,14 +41,17 @@
         total += triple_dot(lefts[1], panel_part(other, panel_kept, 1, part), dims)
         q, half = divmod(part, 2)
         for i in range(ROWS):
-            out[2 * i + (q ^ high), :, half * WIDTH : (half + 1) * WIDTH] = total[
+            out[(2 * i + (q ^ high)) ^ turn, :, half * WIDTH : (half + 1) * WIDTH] = total[
                 i * HALF : (i + 1) * HALF
             ]
 
 
 def panel_part(panel, kept, side, part):
+    turn = 4 * ((lax.rem(lax.axis_index("col"), 2) + side) % 2)
+    start = pl.multiple_of(((2 * part) ^ turn) * BLK, 2 * BLK)
+    blocks = panel[pl.ds(start, 2 * BLK), :]
     return jnp.concatenate(
-        [panel[z * BLK : (z + 1) * BLK, :] * kept[side, z : z + 1, :] for z in (2 * part, 2 * part + 1)],
+        [blocks[h * BLK : (h + 1) * BLK] * kept[side, 2 * part + h : 2 * part + h + 1, :] for h in range(2)],
         axis=0,
     )
 
@@ -55,6 +59,8 @@
 def second_kernel(square, own, other, panel_kept, out):
     high = lax.div(lax.axis_index("layer"), 4)
     core = lax.rem(lax.axis_index("col"), 2)
+    turn = 4 * core
+    first = 2 * (1 - lax.rem(lax.div(lax.axis_index("col"), 2), 2))
     dims = (((1,), (0,)), ((), ()))
     for side, panel in ((0, own), (1, other)):
         total = jnp.zeros((ROWS * HALF, WIDTH), jnp.float32)
@@ -62,14 +68,14 @@
             q, half = divmod(part, 2)
             left = jnp.concatenate(
                 [
-                    square[2 * i + (q ^ high), :, half * WIDTH : (half + 1) * WIDTH]
+                    square[(2 * i + (q ^ high)) ^ turn, :, half * WIDTH : (half + 1) * WIDTH]
                     for i in range(ROWS)
                 ],
                 axis=0,
             )
             total += triple_dot(left, panel_part(panel, panel_kept, side, part), dims)
         for i in range(ROWS):
-            out[i, lax.rem(core + side, 2)] = total[i * HALF : (i + 1) * HALF]
+            out[lax.rem(i + first, ROWS), lax.rem(core + side, 2)] = total[i * HALF : (i + 1) * HALF]
 
 
 def finish_kernel(cube, mirrored, square, purified):
@@ -104,7 +110,7 @@
 
 
 def near_exchange(value):
-    groups = [[chip * 2 + core for chip in range(NEAR)] for core in range(2)]
+    groups = [[(chip ^ 4 * core) * 2 + core for chip in range(NEAR)] for core in range(2)]
     return lax.all_to_all(value, "col", 0, 0, axis_index_groups=groups)
 
 
@@ -155,7 +161,10 @@
     panel_kept = kept_columns(lax.dynamic_index_in_dim(row_groups, row, 0, keepdims=False), col)
     rows_kept = kept_columns(lax.dynamic_index_in_dim(row_groups, layer, 1, keepdims=False), col)
 
-    own = lax.all_to_all(copies(density, LAYERS), "layer", 0, 0).reshape(LAYERS * BLK, WIDTH)
+    lines = [[c * LAYERS + (z ^ 4 * (c % 2)) for z in range(LAYERS)] for c in range(16)]
+    own = lax.all_to_all(
+        copies(density, LAYERS), ("col", "layer"), 0, 0, axis_index_groups=lines
+    ).reshape(LAYERS * BLK, WIDTH)
 
     halves = density.reshape(2, HALF, WIDTH)
     mine = lax.dynamic_index_in_dim(halves, core, 0, keepdims=False)
@@ -192,7 +201,8 @@
         flops=flops,
     )
     homes = [
-        [r * 16 + chip * 2 + c for r in range(ROWS) for c in range(2)] for chip in range(NEAR)
+        [(r + 2 * (1 - chip % 2)) % ROWS * 16 + chip * 2 + c for r in range(ROWS) for c in range(2)]
+        for chip in range(NEAR)
     ]
     cube_terms = cube_terms.reshape(ROWS * 2, HALF, WIDTH)
     cube = lax.all_to_all(cube_terms, ("row", "col"), 0, 0, axis_index_groups=homes)

time: 115 us -> 110 us (0.957)
  the two profiles are of different devices: /device:TPU:1 before, /device:TPU:24 now
where the time goes in v6:
time: 110 us
  starting transfers between devices  36.3 us (33%)
  blocking collectives  34.1 us (31%)
  waiting for transfers between devices  29.8 us (27%)
  local copies, waits for them, and re-layouts  5.42 us (5%)
  Pallas kernels  2.88 us (3%)
    all_to_all x1, blocking collectives, near_exchange(): return lax.all_to_all(value, 'col', 0, 0, axis_index_groups=groups)  18.6 us
    all_gather x1, blocking collectives, body(): rows = lax.all_gather(rows, 'row').reshape(ROWS, 2, HALF, WIDTH)  15.5 us
    ppermute x1, waiting for transfers between devices, mirror_home(): return lax.ppermute(piece, ('row', 'col', 'layer'), pairs)  10.9 us
    all_to_all x1, starting transfers between devices, body(): lax.all_to_all(copies(density, LAYERS), ('col', 'layer'), 0, 0, axis_inde...  10.4 us
    ppermute x3, starting transfers between devices, swap_core(): return lax.ppermute(value, 'col', [(i, i ^ 1) for i in range(16)])  8.28 us
    all_to_all x1, starting transfers between devices, body(): lax.all_to_all(cube_terms, ('row', 'col'), 0, 0, axis_index_groups=homes)  6.77 us
    all_to_all x1, waiting for transfers between devices, body(): lax.all_to_all(copies(density, LAYERS), ('col', 'layer'), 0, 0, axis_inde...  5.76 us
    all_to_all x1, starting transfers between devices, near_exchange(): return lax.all_to_all(value, 'col', 0, 0, axis_index_groups=groups)  5.68 us
  transfers between devices with their start and end apart: 8, of which 8 were waited for; matrix products, arithmetic and copies ran while one was open for 1% of the time, Pallas kernels for 0%

profile of v6, /device:TPU:24, one launch (start us, length us, event | category | flops | bytes accessed | tf_op | source)
XLA Modules:
  0.0 109.5 jit_solution(8386325527716226279)
XLA Ops:
  0.6 2.0 %broadcast_in_dim.8 = f32[8,128,256]{2,1,0:T(8,128)} broadcast(f32[128,256]{1,0:T(8,128)} %param.2), dimensions={1,2} | broadcast | bytes 1179648 | tf_op jit(solution)/shard_map/broadcast_in_dim | solution.py:118
  2.6 10.4 %all-to-all-start = ((f32[8,128,256]{2,1,0:T(8,128)}), f32[8,128,256]{2,1,0:T(8,128)S(1)}, u32[]{:S(2)}, u32[]{:S(2)}) async-start(f32[8,128,256]{2,1,0:T(8,128)} %broadcast_in_dim.8), calls=%async_computation | async-start | bytes 2097152 | tf_op jit(solution)/shard_map/all_to_all | solution.py:165
  13.1 4.4 %collective-permute-start = (f32[64,256]{1,0:T(8,128)S(1)}, f32[64,256]{1,0:T(8,128)S(1)}, u32[]{:S(2)}, u32[]{:S(2)}) collective-permute-start(f32[64,256]{1,0:T(8,128)S(1)} %get-tuple-element.25), channel_id=1, source_target_pairs={{0,8},{8,0},{16,24},{24,16},{32,40},{40,32},{48,56},{56,48},{64,72... | collective-permute-start | bytes 196616 | tf_op jit(solution)/shard_map/ppermute | solution.py:109
  17.5 0.9 collective-permute-done
  18.4 15.5 %all-gather = f32[512,256]{1,0:T(8,128)S(1)} all-gather(f32[128,256]{1,0:T(8,128)S(1)} %pad_maximum_fusion), channel_id=2, replica_groups=mesh['row'=4,'col'=16,'layer'=8] {'row'}, dimensions={0}, use_global_device_ids=true | all-gather | bytes 655360 | tf_op jit(solution)/shard_map/all_gather | solution.py:173
  33.9 5.8 %all-to-all-done = f32[8,128,256]{2,1,0:T(8,128)S(1)} async-done(((f32[8,128,256]{2,1,0:T(8,128)}), f32[8,128,256]{2,1,0:T(8,128)S(1)}, u32[]{:S(2)}, u32[]{:S(2)}) %all-to-all-start) | async-done | bytes 1048608 | tf_op jit(solution)/shard_map/all_to_all | solution.py:165
  39.7 1.9 %collective-permute-start.1 = (f32[1024,256]{1,0:T(8,128)S(1)}, f32[1024,256]{1,0:T(8,128)S(1)}, u32[]{:S(2)}, u32[]{:S(2)}) collective-permute-start(f32[1024,256]{1,0:T(8,128)S(1)} %bitcast.25), channel_id=1, source_target_pairs={{0,8},{8,0},{16,24},{24,16},{32,40},{40,32},{48,56},{56,48},{64,72... | collective-permute-start | bytes 3145736 | tf_op jit(solution)/shard_map/ppermute | solution.py:109
  43.1 1.1 collective-permute-done.1.other
  44.2 1.0 shard_map.41
  45.3 18.6 %all_to_all.20 = f32[8,64,512]{2,1,0:T(8,128)S(1)} all-to-all(f32[8,64,512]{2,1,0:T(8,128)S(1)} %shard_map.41), channel_id=1, replica_groups={{0,16,32,48,64,80,96,112},{72,88,104,120,8,24,40,56},{1,17,33,49,65,81,..., dimensions={0} | all-to-all | bytes 2097152 | tf_op jit(solution)/shard_map/all_to_all | solution.py:114
  64.0 1.1 %broadcast_in_dim.21 = f32[8,64,512]{2,1,0:T(8,128)} broadcast(f32[64,512]{1,0:T(8,128)S(1)} %reduce_sum.9), dimensions={1,2} | broadcast | bytes 1179648 | tf_op jit(solution)/shard_map/broadcast_in_dim | solution.py:118
  65.1 5.7 %all-to-all-start.2 = ((f32[8,64,512]{2,1,0:T(8,128)}), f32[8,64,512]{2,1,0:T(8,128)S(1)}, u32[]{:S(2)}, u32[]{:S(2)}) async-start(f32[8,64,512]{2,1,0:T(8,128)} %broadcast_in_dim.21), calls=%async_computation.2 | async-start | bytes 2097152 | tf_op jit(solution)/shard_map/all_to_all | solution.py:114
  70.9 1.9 %collective-permute-start.2 = (f32[2,64,128]{2,1,0:T(8,128)S(1)}, f32[2,64,128]{2,1,0:T(8,128)S(1)}, u32[]{:S(2)}, u32[]{:S(2)}) collective-permute-start(f32[2,64,128]{2,1,0:T(8,128)S(1)} %pad_maximum_fusion.2), channel_id=1, source_target_pairs={{0,8},{8,0},{16,24},{24,16},{32,40},{40,32},{48,56},{56,48},{64,72... | collective-permute-start | bytes 196616 | tf_op jit(solution)/shard_map/ppermute | solution.py:109
  72.8 1.2 %collective-permute-done.2 = f32[2,64,128]{2,1,0:T(8,128)S(1)} collective-permute-done((f32[2,64,128]{2,1,0:T(8,128)S(1)}, f32[2,64,128]{2,1,0:T(8,128)S(1)}, u32[]{:S(2)}, u32[]{:S(2)}) %collective-permute-start.2) | collective-permute-done | bytes 65568 | tf_op jit(solution)/shard_map/ppermute | solution.py:109
  74.0 1.9 %collective-permute-start.3 = (f32[128,128]{1,0:T(8,128)S(1)}, f32[128,128]{1,0:T(8,128)S(1)}, u32[]{:S(2)}, u32[]{:S(2)}) collective-permute-start(f32[128,128]{1,0:T(8,128)S(1)} %get-tuple-element.15), channel_id=1, source_target_pairs={{0,1},{1,0},{2,3},{3,2},{4,5},{5,4},{6,7},{7,6},{8,9},{9,8},{10,11... | collective-permute-start | bytes 196616 | tf_op jit(solution)/shard_map/ppermute | solution.py:132
  76.0 4.2 %collective-permute-done.3 = f32[128,128]{1,0:T(8,128)S(1)} collective-permute-done((f32[128,128]{1,0:T(8,128)S(1)}, f32[128,128]{1,0:T(8,128)S(1)}, u32[]{:S(2)}, u32[]{:S(2)}) %collective-permute-start.3) | collective-permute-done | bytes 65568 | tf_op jit(solution)/shard_map/ppermute | solution.py:132
  80.2 3.8 %all-to-all-done.2.square = f32[8,64,512]{2,1,0:T(8,128)S(1)} async-done(((f32[8,64,512]{2,1,0:T(8,128)}), f32[8,64,512]{2,1,0:T(8,128)S(1)}, u32[]{:S(2)}, u32[]{:S(2)}) %all-to-all-start.2) | async-done | bytes 1048608 | tf_op jit(solution)/shard_map/all_to_all | solution.py:114
  84.0 1.0 shard_map.42
  85.0 0.8 copy-done
  85.8 6.8 %all-to-all-start.3 = ((f32[8,64,256]{2,1,0:T(8,128)}), f32[8,64,256]{2,1,0:T(8,128)S(1)}, u32[]{:S(2)}, u32[]{:S(2)}) async-start(f32[8,64,256]{2,1,0:T(8,128)} %bitcast.29), calls=%async_computation.3 | async-start | bytes 1048576 | tf_op jit(solution)/shard_map/all_to_all | solution.py:208
  92.6 3.2 %collective-permute-start.4 = (f32[256,128]{1,0:T(8,128)S(1)}, f32[256,128]{1,0:T(8,128)S(1)}, u32[]{:S(2)}, u32[]{:S(2)}) collective-permute-start(f32[256,128]{1,0:T(8,128)S(1)} %maximum_select_fusion.1), channel_id=1, source_target_pairs={{0,0},{1,1},{2,10},{3,11},{4,20},{5,21},{6,30},{7,31},{8,2},{9,3},... | collective-permute-start | bytes 393224 | tf_op jit(solution)/shard_map/ppermute | solution.py:128
  95.8 10.9 %collective-permute-done.4.mirrored = f32[256,128]{1,0:T(8,128)S(1)} collective-permute-done((f32[256,128]{1,0:T(8,128)S(1)}, f32[256,128]{1,0:T(8,128)S(1)}, u32[]{:S(2)}, u32[]{:S(2)}) %collective-permute-start.4) | collective-permute-done | bytes 131104 | tf_op jit(solution)/shard_map/ppermute | solution.py:128
  106.7 2.0 %all-to-all-done.3.cube = f32[8,64,256]{2,1,0:T(8,128)S(1)} async-done(((f32[8,64,256]{2,1,0:T(8,128)}), f32[8,64,256]{2,1,0:T(8,128)S(1)}, u32[]{:S(2)}, u32[]{:S(2)}) %all-to-all-start.3) | async-done | bytes 524320 | tf_op jit(solution)/shard_map/all_to_all | solution.py:208
  108.7 0.8 shard_map.43
  (27 shorter events, 1.7 us)
Async XLA Ops:
  2.6 10.5 %copy-start.1 = (f32[128,256]{1,0:T(8,128)S(1)}, f32[128,256]{1,0:T(8,128)}, u32[]{:S(2)}) copy-start(f32[128,256]{1,0:T(8,128)} %param.2) | copy-start | bytes 393220
  2.6 37.1 %all-to-all-start = ((f32[8,128,256]{2,1,0:T(8,128)}), f32[8,128,256]{2,1,0:T(8,128)S(1)}, u32[]{:S(2)}, u32[]{:S(2)}) async-start(f32[8,128,256]{2,1,0:T(8,128)} %broadcast_in_dim.8), calls=%async_computation | async-start | bytes 2097152 | tf_op jit(solution)/shard_map/all_to_all | solution.py:165
  13.1 5.3 %collective-permute-start = (f32[64,256]{1,0:T(8,128)S(1)}, f32[64,256]{1,0:T(8,128)S(1)}, u32[]{:S(2)}, u32[]{:S(2)}) collective-permute-start(f32[64,256]{1,0:T(8,128)S(1)} %get-tuple-element.25), channel_id=1, source_target_pairs={{0,8},{8,0},{16,24},{24,16},{32,40},{40,32},{48,56},{56,48},{64,72... | collective-permute-start | bytes 196616 | tf_op jit(solution)/shard_map/ppermute | solution.py:109
  39.7 4.5 %collective-permute-start.1 = (f32[1024,256]{1,0:T(8,128)S(1)}, f32[1024,256]{1,0:T(8,128)S(1)}, u32[]{:S(2)}, u32[]{:S(2)}) collective-permute-start(f32[1024,256]{1,0:T(8,128)S(1)} %bitcast.25), channel_id=1, source_target_pairs={{0,8},{8,0},{16,24},{24,16},{32,40},{40,32},{48,56},{56,48},{64,72... | collective-permute-start | bytes 3145736 | tf_op jit(solution)/shard_map/ppermute | solution.py:109
  41.6 0.7 copy-start.2
  65.1 18.9 %all-to-all-start.2 = ((f32[8,64,512]{2,1,0:T(8,128)}), f32[8,64,512]{2,1,0:T(8,128)S(1)}, u32[]{:S(2)}, u32[]{:S(2)}) async-start(f32[8,64,512]{2,1,0:T(8,128)} %broadcast_in_dim.21), calls=%async_computation.2 | async-start | bytes 2097152 | tf_op jit(solution)/shard_map/all_to_all | solution.py:114
  70.9 3.1 %collective-permute-start.2 = (f32[2,64,128]{2,1,0:T(8,128)S(1)}, f32[2,64,128]{2,1,0:T(8,128)S(1)}, u32[]{:S(2)}, u32[]{:S(2)}) collective-permute-start(f32[2,64,128]{2,1,0:T(8,128)S(1)} %pad_maximum_fusion.2), channel_id=1, source_target_pairs={{0,8},{8,0},{16,24},{24,16},{32,40},{40,32},{48,56},{56,48},{64,72... | collective-permute-start | bytes 196616 | tf_op jit(solution)/shard_map/ppermute | solution.py:109
  74.0 6.2 %collective-permute-start.3 = (f32[128,128]{1,0:T(8,128)S(1)}, f32[128,128]{1,0:T(8,128)S(1)}, u32[]{:S(2)}, u32[]{:S(2)}) collective-permute-start(f32[128,128]{1,0:T(8,128)S(1)} %get-tuple-element.15), channel_id=1, source_target_pairs={{0,1},{1,0},{2,3},{3,2},{4,5},{5,4},{6,7},{7,6},{8,9},{9,8},{10,11... | collective-permute-start | bytes 196616 | tf_op jit(solution)/shard_map/ppermute | solution.py:132
  85.0 0.8 copy-start
  85.8 22.9 %all-to-all-start.3 = ((f32[8,64,256]{2,1,0:T(8,128)}), f32[8,64,256]{2,1,0:T(8,128)S(1)}, u32[]{:S(2)}, u32[]{:S(2)}) async-start(f32[8,64,256]{2,1,0:T(8,128)} %bitcast.29), calls=%async_computation.3 | async-start | bytes 1048576 | tf_op jit(solution)/shard_map/all_to_all | solution.py:208
  92.6 14.1 %collective-permute-start.4 = (f32[256,128]{1,0:T(8,128)S(1)}, f32[256,128]{1,0:T(8,128)S(1)}, u32[]{:S(2)}, u32[]{:S(2)}) collective-permute-start(f32[256,128]{1,0:T(8,128)S(1)} %maximum_select_fusion.1), channel_id=1, source_target_pairs={{0,0},{1,1},{2,10},{3,11},{4,20},{5,21},{6,30},{7,31},{8,2},{9,3},... | collective-permute-start | bytes 393224 | tf_op jit(solution)/shard_map/ppermute | solution.py:128

commit v7 on v6

--- a/solution.py
+++ b/solution.py
@@ -26,19 +26,24 @@
     return total + lax.dot_general(left_high, right_high, dims, preferred_element_type=jnp.float32)
 
 
-def first_kernel(rows, own, other, rows_kept, panel_kept, out):
+def first_terms(rows, panel, rows_kept, panel_kept, side, part):
+    left = jnp.concatenate(
+        [rows[i, side] * rows_kept[side, i : i + 1, :] for i in range(ROWS)], axis=0
+    )
+    dims = (((1,), (1,)), ((), ()))
+    return triple_dot(left, panel_part(panel, panel_kept, side, part), dims)
+
+
+def own_kernel(rows, own, rows_kept, panel_kept, out):
+    for part in range(4):
+        out[part] = first_terms(rows, own, rows_kept, panel_kept, 0, part)
+
+
+def first_kernel(rows, begun, other, rows_kept, panel_kept, out):
     high = lax.div(lax.axis_index("layer"), 4)
     turn = 4 * lax.rem(lax.axis_index("col"), 2)
-    lefts = [
-        jnp.concatenate(
-            [rows[i, side] * rows_kept[side, i : i + 1, :] for i in range(ROWS)], axis=0
-        )
-        for side in range(2)
-    ]
-    dims = (((1,), (1,)), ((), ()))
     for part in range(4):
-        total = triple_dot(lefts[0], panel_part(own, panel_kept, 0, part), dims)
-        total += triple_dot(lefts[1], panel_part(other, panel_kept, 1, part), dims)
+        total = begun[part] + first_terms(rows, other, rows_kept, panel_kept, 1, part)
         q, half = divmod(part, 2)
         for i in range(ROWS):
             out[(2 * i + (q ^ high)) ^ turn, :, half * WIDTH : (half + 1) * WIDTH] = total[
@@ -78,13 +83,15 @@
             out[lax.rem(i + first, ROWS), lax.rem(core + side, 2)] = total[i * HALF : (i + 1) * HALF]
 
 
-def finish_kernel(cube, mirrored, square, purified):
-    home = mirrored[...].T
-    square[...] = home
+def home_kernel(mirrored, square):
+    square[...] = mirrored[...].T
+
+
+def finish_kernel(cube, square, purified):
     for c in range(2):
         rows = slice(c * HALF, (c + 1) * HALF)
         total = (cube[c] + cube[2 + c]) + (cube[4 + c] + cube[6 + c])
-        purified[rows] = 3.0 * home[rows] - 2.0 * total
+        purified[rows] = 3.0 * square[rows] - 2.0 * total
 
 
 def call(kernel, shapes, *operands, flops):
@@ -175,15 +182,24 @@
     own, rows = lax.optimization_barrier((own, rows))
     other = swap_core(own)
     flops = 6 * 256 * 512 * 1024
+    (begun,) = call(
+        own_kernel,
+        [(4, ROWS * HALF, WIDTH)],
+        rows,
+        own,
+        rows_kept,
+        panel_kept,
+        flops=flops // 2,
+    )
     (square_terms,) = call(
         first_kernel,
         [(NEAR, HALF, 2 * WIDTH)],
         rows,
-        own,
+        begun,
         other,
         rows_kept,
         panel_kept,
-        flops=flops,
+        flops=flops // 2,
     )
     square_piece = jnp.sum(near_exchange(square_terms), axis=0)
     square_rows = near_exchange(copies(square_piece, NEAR))
@@ -206,10 +222,9 @@
     ]
     cube_terms = cube_terms.reshape(ROWS * 2, HALF, WIDTH)
     cube = lax.all_to_all(cube_terms, ("row", "col"), 0, 0, axis_index_groups=homes)
-    cube, mirrored = lax.optimization_barrier((cube, mirrored))
-    square, purified = call(
-        finish_kernel, [(BLK, WIDTH)] * 2, cube, mirrored, flops=16 * BLK * WIDTH
-    )
+    (square,) = call(home_kernel, [(BLK, WIDTH)], mirrored, flops=BLK * WIDTH)
+    cube, square = lax.optimization_barrier((cube, square))
+    (purified,) = call(finish_kernel, [(BLK, WIDTH)], cube, square, flops=8 * BLK * WIDTH)
     return (square, purified)
 
 

time: 110 us -> 114 us (1.036)
  the two profiles are of different devices: /device:TPU:24 before, /device:TPU:10 now
where the time goes in v7:
time: 114 us; the launch traced here: 113 us
  starting transfers between devices  40.5 us (36%)
  blocking collectives  36.6 us (32%)
  waiting for transfers between devices  23.7 us (21%)
  Pallas kernels  5.76 us (5%)
  local copies, waits for them, and re-layouts  5.55 us (5%)
    all_gather x1, blocking collectives, body(): rows = lax.all_gather(rows, 'row').reshape(ROWS, 2, HALF, WIDTH)  18.4 us
    all_to_all x1, blocking collectives, near_exchange(): return lax.all_to_all(value, 'col', 0, 0, axis_index_groups=groups)  18.2 us
    all_to_all x1, starting transfers between devices, body(): lax.all_to_all(copies(density, LAYERS), ('col', 'layer'), 0, 0, axis_inde...  10.4 us
    ppermute x3, starting transfers between devices, swap_core(): return lax.ppermute(value, 'col', [(i, i ^ 1) for i in range(16)])  8.26 us
    ppermute x1, waiting for transfers between devices, mirror_home(): return lax.ppermute(piece, ('row', 'col', 'layer'), pairs)  7.9 us
    ppermute x1, starting transfers between devices, mirror_home(): return lax.ppermute(piece, ('row', 'col', 'layer'), pairs)  6.98 us
    all_to_all x1, starting transfers between devices, body(): lax.all_to_all(cube_terms, ('row', 'col'), 0, 0, axis_index_groups=homes)  6.83 us
    all_to_all x1, starting transfers between devices, near_exchange(): return lax.all_to_all(value, 'col', 0, 0, axis_index_groups=groups)  6.05 us
  transfers between devices with their start and end apart: 8, of which 8 were waited for; matrix products, arithmetic and copies ran while one was open for 1% of the time, Pallas kernels for 1%

profile of v7, /device:TPU:10, one launch (start us, length us, event | category | flops | bytes accessed | tf_op | source)
XLA Modules:
  0.0 113.1 jit_solution(16430777663990642129)
XLA Ops:
  0.6 2.0 %broadcast_in_dim.8 = f32[8,128,256]{2,1,0:T(8,128)} broadcast(f32[128,256]{1,0:T(8,128)} %param.2), dimensions={1,2} | broadcast | bytes 1179648 | tf_op jit(solution)/shard_map/broadcast_in_dim | solution.py:125
  2.6 10.4 %all-to-all-start = ((f32[8,128,256]{2,1,0:T(8,128)}), f32[8,128,256]{2,1,0:T(8,128)S(1)}, u32[]{:S(2)}, u32[]{:S(2)}) async-start(f32[8,128,256]{2,1,0:T(8,128)} %broadcast_in_dim.8), calls=%async_computation | async-start | bytes 2097152 | tf_op jit(solution)/shard_map/all_to_all | solution.py:172
  13.1 4.4 %collective-permute-start = (f32[64,256]{1,0:T(8,128)S(1)}, f32[64,256]{1,0:T(8,128)S(1)}, u32[]{:S(2)}, u32[]{:S(2)}) collective-permute-start(f32[64,256]{1,0:T(8,128)S(1)} %get-tuple-element.25), channel_id=1, source_target_pairs={{0,8},{8,0},{16,24},{24,16},{32,40},{40,32},{48,56},{56,48},{64,72... | collective-permute-start | bytes 196616 | tf_op jit(solution)/shard_map/ppermute | solution.py:116
  17.5 0.9 collective-permute-done
  18.4 18.4 %all-gather = f32[512,256]{1,0:T(8,128)S(1)} all-gather(f32[128,256]{1,0:T(8,128)S(1)} %pad_maximum_fusion), channel_id=2, replica_groups=mesh['row'=4,'col'=16,'layer'=8] {'row'}, dimensions={0}, use_global_device_ids=true | all-gather | bytes 655360 | tf_op jit(solution)/shard_map/all_gather | solution.py:180
  36.8 2.9 %all-to-all-done = f32[8,128,256]{2,1,0:T(8,128)S(1)} async-done(((f32[8,128,256]{2,1,0:T(8,128)}), f32[8,128,256]{2,1,0:T(8,128)S(1)}, u32[]{:S(2)}, u32[]{:S(2)}) %all-to-all-start) | async-done | bytes 1048608 | tf_op jit(solution)/shard_map/all_to_all | solution.py:172
  39.7 1.9 %collective-permute-start.1 = (f32[1024,256]{1,0:T(8,128)S(1)}, f32[1024,256]{1,0:T(8,128)S(1)}, u32[]{:S(2)}, u32[]{:S(2)}) collective-permute-start(f32[1024,256]{1,0:T(8,128)S(1)} %bitcast.25), channel_id=1, source_target_pairs={{0,8},{8,0},{16,24},{24,16},{32,40},{40,32},{48,56},{56,48},{64,72... | collective-permute-start | bytes 3145736 | tf_op jit(solution)/shard_map/ppermute | solution.py:116
  41.6 0.7 copy-done.2
  44.9 18.2 %all_to_all.20 = f32[8,64,512]{2,1,0:T(8,128)S(1)} all-to-all(f32[8,64,512]{2,1,0:T(8,128)S(1)} %shard_map.42), channel_id=1, replica_groups={{0,16,32,48,64,80,96,112},{72,88,104,120,8,24,40,56},{1,17,33,49,65,81,..., dimensions={0} | all-to-all | bytes 2097152 | tf_op jit(solution)/shard_map/all_to_all | solution.py:121
  63.2 1.1 broadcast_in_dim.21
  64.3 6.1 %all-to-all-start.2 = ((f32[8,64,512]{2,1,0:T(8,128)}), f32[8,64,512]{2,1,0:T(8,128)}, u32[]{:S(2)}, u32[]{:S(2)}) async-start(f32[8,64,512]{2,1,0:T(8,128)} %broadcast_in_dim.21), calls=%async_computation.2 | async-start | bytes 2097152 | tf_op jit(solution)/shard_map/all_to_all | solution.py:121
  70.5 1.9 %collective-permute-start.2 = (f32[2,64,128]{2,1,0:T(8,128)S(1)}, f32[2,64,128]{2,1,0:T(8,128)S(1)}, u32[]{:S(2)}, u32[]{:S(2)}) collective-permute-start(f32[2,64,128]{2,1,0:T(8,128)S(1)} %pad_maximum_fusion.2), channel_id=1, source_target_pairs={{0,8},{8,0},{16,24},{24,16},{32,40},{40,32},{48,56},{56,48},{64,72... | collective-permute-start | bytes 196616 | tf_op jit(solution)/shard_map/ppermute | solution.py:116
  72.4 1.2 %collective-permute-done.2 = f32[2,64,128]{2,1,0:T(8,128)S(1)} collective-permute-done((f32[2,64,128]{2,1,0:T(8,128)S(1)}, f32[2,64,128]{2,1,0:T(8,128)S(1)}, u32[]{:S(2)}, u32[]{:S(2)}) %collective-permute-start.2) | collective-permute-done | bytes 65568 | tf_op jit(solution)/shard_map/ppermute | solution.py:116
  73.6 1.9 %collective-permute-start.3 = (f32[128,128]{1,0:T(8,128)S(1)}, f32[128,128]{1,0:T(8,128)S(1)}, u32[]{:S(2)}, u32[]{:S(2)}) collective-permute-start(f32[128,128]{1,0:T(8,128)S(1)} %get-tuple-element.15), channel_id=1, source_target_pairs={{0,1},{1,0},{2,3},{3,2},{4,5},{5,4},{6,7},{7,6},{8,9},{9,8},{10,11... | collective-permute-start | bytes 196616 | tf_op jit(solution)/shard_map/ppermute | solution.py:139
  75.6 4.2 %collective-permute-done.3 = f32[128,128]{1,0:T(8,128)S(1)} collective-permute-done((f32[128,128]{1,0:T(8,128)S(1)}, f32[128,128]{1,0:T(8,128)S(1)}, u32[]{:S(2)}, u32[]{:S(2)}) %collective-permute-start.3) | collective-permute-done | bytes 65568 | tf_op jit(solution)/shard_map/ppermute | solution.py:139
  79.8 3.2 %all-to-all-done.2.square = f32[8,64,512]{2,1,0:T(8,128)} async-done(((f32[8,64,512]{2,1,0:T(8,128)}), f32[8,64,512]{2,1,0:T(8,128)}, u32[]{:S(2)}, u32[]{:S(2)}) %all-to-all-start.2) | async-done | bytes 1048608 | tf_op jit(solution)/shard_map/all_to_all | solution.py:121
  83.0 3.0 %shard_map.43 = f32[4,2,64,256]{3,2,1,0:T(8,128)} custom-call(f32[8,64,512]{2,1,0:T(8,128)} %all-to-all-done.2.square, f32[1024,256]{1,0:T(8,128)S(1)} %bitcast.27, f32[1024,256]{1,0:T(8,128)S(1)} %collective-permute-done.1.other, f32[2,8,256]{2,1,0:T(8,128)S(1)} %broadcast_bitcast_fusion.panel_kept), custom_call_target="tpu_custom_call" | custom-call | flops 805306368 | bytes 1048576 | tf_op jit(solution)/shard_map/pallas_call | solution.py:98
  86.0 6.8 %all-to-all-start.3 = ((f32[8,64,256]{2,1,0:T(8,128)}), f32[8,64,256]{2,1,0:T(8,128)S(1)}, u32[]{:S(2)}, u32[]{:S(2)}) async-start(f32[8,64,256]{2,1,0:T(8,128)} %bitcast.15), calls=%async_computation.3 | async-start | bytes 1048576 | tf_op jit(solution)/shard_map/all_to_all | solution.py:224
  92.9 7.0 %collective-permute-start.4 = (f32[256,128]{1,0:T(8,128)S(1)}, f32[256,128]{1,0:T(8,128)S(1)}, u32[]{:S(2)}, u32[]{:S(2)}) collective-permute-start(f32[256,128]{1,0:T(8,128)S(1)} %maximum_select_fusion.1), channel_id=1, source_target_pairs={{0,0},{1,1},{2,10},{3,11},{4,20},{5,21},{6,30},{7,31},{8,2},{9,3},... | collective-permute-start | bytes 393224 | tf_op jit(solution)/shard_map/ppermute | solution.py:135
  99.8 7.9 %collective-permute-done.4.mirrored = f32[256,128]{1,0:T(8,128)S(1)} collective-permute-done((f32[256,128]{1,0:T(8,128)S(1)}, f32[256,128]{1,0:T(8,128)S(1)}, u32[]{:S(2)}, u32[]{:S(2)}) %collective-permute-start.4) | collective-permute-done | bytes 131104 | tf_op jit(solution)/shard_map/ppermute | solution.py:135
  107.7 0.8 shard_map.44.square
  108.5 3.0 %all-to-all-done.3.cube = f32[8,64,256]{2,1,0:T(8,128)S(1)} async-done(((f32[8,64,256]{2,1,0:T(8,128)}), f32[8,64,256]{2,1,0:T(8,128)S(1)}, u32[]{:S(2)}, u32[]{:S(2)}) %all-to-all-start.3) | async-done | bytes 524320 | tf_op jit(solution)/shard_map/all_to_all | solution.py:224
  111.5 0.9 copy-done
  112.4 0.7 shard_map.45
  (29 shorter events, 2.7 us)
Async XLA Ops:
  2.6 10.5 %copy-start.1 = (f32[128,256]{1,0:T(8,128)S(1)}, f32[128,256]{1,0:T(8,128)}, u32[]{:S(2)}) copy-start(f32[128,256]{1,0:T(8,128)} %param.2) | copy-start | bytes 393220
  2.6 37.1 %all-to-all-start = ((f32[8,128,256]{2,1,0:T(8,128)}), f32[8,128,256]{2,1,0:T(8,128)S(1)}, u32[]{:S(2)}, u32[]{:S(2)}) async-start(f32[8,128,256]{2,1,0:T(8,128)} %broadcast_in_dim.8), calls=%async_computation | async-start | bytes 2097152 | tf_op jit(solution)/shard_map/all_to_all | solution.py:172
  13.1 5.3 %collective-permute-start = (f32[64,256]{1,0:T(8,128)S(1)}, f32[64,256]{1,0:T(8,128)S(1)}, u32[]{:S(2)}, u32[]{:S(2)}) collective-permute-start(f32[64,256]{1,0:T(8,128)S(1)} %get-tuple-element.25), channel_id=1, source_target_pairs={{0,8},{8,0},{16,24},{24,16},{32,40},{40,32},{48,56},{56,48},{64,72... | collective-permute-start | bytes 196616 | tf_op jit(solution)/shard_map/ppermute | solution.py:116
  39.7 4.5 %collective-permute-start.1 = (f32[1024,256]{1,0:T(8,128)S(1)}, f32[1024,256]{1,0:T(8,128)S(1)}, u32[]{:S(2)}, u32[]{:S(2)}) collective-permute-start(f32[1024,256]{1,0:T(8,128)S(1)} %bitcast.25), channel_id=1, source_target_pairs={{0,8},{8,0},{16,24},{24,16},{32,40},{40,32},{48,56},{56,48},{64,72... | collective-permute-start | bytes 3145736 | tf_op jit(solution)/shard_map/ppermute | solution.py:116
  41.6 0.7 copy-start.2
  64.3 18.6 %all-to-all-start.2 = ((f32[8,64,512]{2,1,0:T(8,128)}), f32[8,64,512]{2,1,0:T(8,128)}, u32[]{:S(2)}, u32[]{:S(2)}) async-start(f32[8,64,512]{2,1,0:T(8,128)} %broadcast_in_dim.21), calls=%async_computation.2 | async-start | bytes 2097152 | tf_op jit(solution)/shard_map/all_to_all | solution.py:121
  70.5 3.1 %collective-permute-start.2 = (f32[2,64,128]{2,1,0:T(8,128)S(1)}, f32[2,64,128]{2,1,0:T(8,128)S(1)}, u32[]{:S(2)}, u32[]{:S(2)}) collective-permute-start(f32[2,64,128]{2,1,0:T(8,128)S(1)} %pad_maximum_fusion.2), channel_id=1, source_target_pairs={{0,8},{8,0},{16,24},{24,16},{32,40},{40,32},{48,56},{56,48},{64,72... | collective-permute-start | bytes 196616 | tf_op jit(solution)/shard_map/ppermute | solution.py:116
  73.6 6.2 %collective-permute-start.3 = (f32[128,128]{1,0:T(8,128)S(1)}, f32[128,128]{1,0:T(8,128)S(1)}, u32[]{:S(2)}, u32[]{:S(2)}) collective-permute-start(f32[128,128]{1,0:T(8,128)S(1)} %get-tuple-element.15), channel_id=1, source_target_pairs={{0,1},{1,0},{2,3},{3,2},{4,5},{5,4},{6,7},{7,6},{8,9},{9,8},{10,11... | collective-permute-start | bytes 196616 | tf_op jit(solution)/shard_map/ppermute | solution.py:139
  86.0 25.4 %all-to-all-start.3 = ((f32[8,64,256]{2,1,0:T(8,128)}), f32[8,64,256]{2,1,0:T(8,128)S(1)}, u32[]{:S(2)}, u32[]{:S(2)}) async-start(f32[8,64,256]{2,1,0:T(8,128)} %bitcast.15), calls=%async_computation.3 | async-start | bytes 1048576 | tf_op jit(solution)/shard_map/all_to_all | solution.py:224
  92.9 14.9 %collective-permute-start.4 = (f32[256,128]{1,0:T(8,128)S(1)}, f32[256,128]{1,0:T(8,128)S(1)}, u32[]{:S(2)}, u32[]{:S(2)}) collective-permute-start(f32[256,128]{1,0:T(8,128)S(1)} %maximum_select_fusion.1), channel_id=1, source_target_pairs={{0,0},{1,1},{2,10},{3,11},{4,20},{5,21},{6,30},{7,31},{8,2},{9,3},... | collective-permute-start | bytes 393224 | tf_op jit(solution)/shard_map/ppermute | solution.py:135
  111.5 0.9 copy-start

commit v8 on v6

--- a/solution.py
+++ b/solution.py
@@ -47,7 +47,7 @@
 
 
 def panel_part(panel, kept, side, part):
-    turn = 4 * ((lax.rem(lax.axis_index("col"), 2) + side) % 2)
+    turn = 4 * ((lax.rem(lax.axis_index("col"), 2) + side + 1) % 2)
     start = pl.multiple_of(((2 * part) ^ turn) * BLK, 2 * BLK)
     blocks = panel[pl.ds(start, 2 * BLK), :]
     return jnp.concatenate(
@@ -161,7 +161,7 @@
     panel_kept = kept_columns(lax.dynamic_index_in_dim(row_groups, row, 0, keepdims=False), col)
     rows_kept = kept_columns(lax.dynamic_index_in_dim(row_groups, layer, 1, keepdims=False), col)
 
-    lines = [[c * LAYERS + (z ^ 4 * (c % 2)) for z in range(LAYERS)] for c in range(16)]
+    lines = [[c * LAYERS + (z ^ 4 * (1 - c % 2)) for z in range(LAYERS)] for c in range(16)]
     own = lax.all_to_all(
         copies(density, LAYERS), ("col", "layer"), 0, 0, axis_index_groups=lines
     ).reshape(LAYERS * BLK, WIDTH)

time: 110 us -> 110 us (level)
  the two profiles are of different devices: /device:TPU:24 before, /device:TPU:10 now
where the time goes in v8:
time: 110 us; the launch traced here: 109 us
  starting transfers between devices  44.5 us (40%)
  blocking collectives  37.5 us (34%)
  waiting for transfers between devices  18 us (16%)
  local copies, waits for them, and re-layouts  5.41 us (5%)
  Pallas kernels  2.87 us (3%)
    all_to_all x1, blocking collectives, near_exchange(): return lax.all_to_all(value, 'col', 0, 0, axis_index_groups=groups)  19 us
    all_gather x1, blocking collectives, body(): rows = lax.all_gather(rows, 'row').reshape(ROWS, 2, HALF, WIDTH)  18.5 us
    all_to_all x1, starting transfers between devices, body(): lax.all_to_all(copies(density, LAYERS), ('col', 'layer'), 0, 0, axis_inde...  13.7 us
    ppermute x1, starting transfers between devices, mirror_home(): return lax.ppermute(piece, ('row', 'col', 'layer'), pairs)  9.89 us
    all_to_all x1, starting transfers between devices, near_exchange(): return lax.all_to_all(value, 'col', 0, 0, axis_index_groups=groups)  6.15 us
    ppermute x3, starting transfers between devices, swap_core(): return lax.ppermute(value, 'col', [(i, i ^ 1) for i in range(16)])  6.03 us
    all_to_all x1, starting transfers between devices, body(): lax.all_to_all(cube_terms, ('row', 'col'), 0, 0, axis_index_groups=homes)  5.66 us
    ppermute x1, waiting for transfers between devices, mirror_home(): return lax.ppermute(piece, ('row', 'col', 'layer'), pairs)  5.28 us
  transfers between devices with their start and end apart: 8, of which 7 were waited for; matrix products, arithmetic and copies ran while one was open for 1% of the time, Pallas kernels for 0%

profile of v8, /device:TPU:10, one launch (start us, length us, event | category | flops | bytes accessed | tf_op | source)
XLA Modules:
  0.0 109.2 jit_solution(11889907922456682606)
XLA Ops:
  0.6 2.0 %broadcast_in_dim.8 = f32[8,128,256]{2,1,0:T(8,128)} broadcast(f32[128,256]{1,0:T(8,128)} %param.2), dimensions={1,2} | broadcast | bytes 1179648 | tf_op jit(solution)/shard_map/broadcast_in_dim | solution.py:118
  2.6 13.7 %all-to-all-start = ((f32[8,128,256]{2,1,0:T(8,128)}), f32[8,128,256]{2,1,0:T(8,128)S(1)}, u32[]{:S(2)}, u32[]{:S(2)}) async-start(f32[8,128,256]{2,1,0:T(8,128)} %broadcast_in_dim.8), calls=%async_computation | async-start | bytes 2097152 | tf_op jit(solution)/shard_map/all_to_all | solution.py:165
  16.3 1.9 %collective-permute-start = (f32[64,256]{1,0:T(8,128)S(1)}, f32[64,256]{1,0:T(8,128)S(1)}, u32[]{:S(2)}, u32[]{:S(2)}) collective-permute-start(f32[64,256]{1,0:T(8,128)S(1)} %get-tuple-element.25), channel_id=1, source_target_pairs={{0,8},{8,0},{16,24},{24,16},{32,40},{40,32},{48,56},{56,48},{64,72... | collective-permute-start | bytes 196616 | tf_op jit(solution)/shard_map/ppermute | solution.py:109
  18.3 1.2 %collective-permute-done = f32[64,256]{1,0:T(8,128)S(1)} collective-permute-done((f32[64,256]{1,0:T(8,128)S(1)}, f32[64,256]{1,0:T(8,128)S(1)}, u32[]{:S(2)}, u32[]{:S(2)}) %collective-permute-start) | collective-permute-done | bytes 65568 | tf_op jit(solution)/shard_map/ppermute | solution.py:109
  19.5 18.5 %all-gather = f32[512,256]{1,0:T(8,128)S(1)} all-gather(f32[128,256]{1,0:T(8,128)S(1)} %pad_maximum_fusion), channel_id=2, replica_groups=mesh['row'=4,'col'=16,'layer'=8] {'row'}, dimensions={0}, use_global_device_ids=true | all-gather | bytes 655360 | tf_op jit(solution)/shard_map/all_gather | solution.py:173
  38.0 2.2 %collective-permute-start.1 = (f32[1024,256]{1,0:T(8,128)S(1)}, f32[1024,256]{1,0:T(8,128)S(1)}, u32[]{:S(2)}, u32[]{:S(2)}) collective-permute-start(f32[1024,256]{1,0:T(8,128)S(1)} %bitcast.25), channel_id=1, source_target_pairs={{0,8},{8,0},{16,24},{24,16},{32,40},{40,32},{48,56},{56,48},{64,72... | collective-permute-start | bytes 3145736 | tf_op jit(solution)/shard_map/ppermute | solution.py:109
  40.2 0.7 copy-done.2
  41.7 0.8 collective-permute-done.1.other
  42.6 1.0 shard_map.41
  43.6 19.0 %all_to_all.20 = f32[8,64,512]{2,1,0:T(8,128)S(1)} all-to-all(f32[8,64,512]{2,1,0:T(8,128)S(1)} %shard_map.41), channel_id=1, replica_groups={{0,16,32,48,64,80,96,112},{72,88,104,120,8,24,40,56},{1,17,33,49,65,81,..., dimensions={0} | all-to-all | bytes 2097152 | tf_op jit(solution)/shard_map/all_to_all | solution.py:114
  62.6 1.1 %broadcast_in_dim.21 = f32[8,64,512]{2,1,0:T(8,128)} broadcast(f32[64,512]{1,0:T(8,128)S(1)} %reduce_sum.9), dimensions={1,2} | broadcast | bytes 1179648 | tf_op jit(solution)/shard_map/broadcast_in_dim | solution.py:118
  63.8 6.2 %all-to-all-start.2 = ((f32[8,64,512]{2,1,0:T(8,128)}), f32[8,64,512]{2,1,0:T(8,128)S(1)}, u32[]{:S(2)}, u32[]{:S(2)}) async-start(f32[8,64,512]{2,1,0:T(8,128)} %broadcast_in_dim.21), calls=%async_computation.2 | async-start | bytes 2097152 | tf_op jit(solution)/shard_map/all_to_all | solution.py:114
  70.0 1.9 %collective-permute-start.2 = (f32[2,64,128]{2,1,0:T(8,128)S(1)}, f32[2,64,128]{2,1,0:T(8,128)S(1)}, u32[]{:S(2)}, u32[]{:S(2)}) collective-permute-start(f32[2,64,128]{2,1,0:T(8,128)S(1)} %pad_maximum_fusion.2), channel_id=1, source_target_pairs={{0,8},{8,0},{16,24},{24,16},{32,40},{40,32},{48,56},{56,48},{64,72... | collective-permute-start | bytes 196616 | tf_op jit(solution)/shard_map/ppermute | solution.py:109
  71.9 1.2 %collective-permute-done.2 = f32[2,64,128]{2,1,0:T(8,128)S(1)} collective-permute-done((f32[2,64,128]{2,1,0:T(8,128)S(1)}, f32[2,64,128]{2,1,0:T(8,128)S(1)}, u32[]{:S(2)}, u32[]{:S(2)}) %collective-permute-start.2) | collective-permute-done | bytes 65568 | tf_op jit(solution)/shard_map/ppermute | solution.py:109
  73.2 3.1 %collective-permute-start.3 = (f32[128,128]{1,0:T(8,128)S(1)}, f32[128,128]{1,0:T(8,128)S(1)}, u32[]{:S(2)}, u32[]{:S(2)}) collective-permute-start(f32[128,128]{1,0:T(8,128)S(1)} %get-tuple-element.15), channel_id=1, source_target_pairs={{0,1},{1,0},{2,3},{3,2},{4,5},{5,4},{6,7},{7,6},{8,9},{9,8},{10,11... | collective-permute-start | bytes 196616 | tf_op jit(solution)/shard_map/ppermute | solution.py:132
  76.3 3.1 %collective-permute-done.3 = f32[128,128]{1,0:T(8,128)S(1)} collective-permute-done((f32[128,128]{1,0:T(8,128)S(1)}, f32[128,128]{1,0:T(8,128)S(1)}, u32[]{:S(2)}, u32[]{:S(2)}) %collective-permute-start.3) | collective-permute-done | bytes 65568 | tf_op jit(solution)/shard_map/ppermute | solution.py:132
  79.3 3.0 %all-to-all-done.2.square = f32[8,64,512]{2,1,0:T(8,128)S(1)} async-done(((f32[8,64,512]{2,1,0:T(8,128)}), f32[8,64,512]{2,1,0:T(8,128)S(1)}, u32[]{:S(2)}, u32[]{:S(2)}) %all-to-all-start.2) | async-done | bytes 1048608 | tf_op jit(solution)/shard_map/all_to_all | solution.py:114
  82.3 1.0 shard_map.42
  83.4 0.8 copy-done
  84.2 5.7 %all-to-all-start.3 = ((f32[8,64,256]{2,1,0:T(8,128)}), f32[8,64,256]{2,1,0:T(8,128)S(1)}, u32[]{:S(2)}, u32[]{:S(2)}) async-start(f32[8,64,256]{2,1,0:T(8,128)} %bitcast.29), calls=%async_computation.3 | async-start | bytes 1048576 | tf_op jit(solution)/shard_map/all_to_all | solution.py:208
  89.8 9.9 %collective-permute-start.4 = (f32[256,128]{1,0:T(8,128)S(1)}, f32[256,128]{1,0:T(8,128)S(1)}, u32[]{:S(2)}, u32[]{:S(2)}) collective-permute-start(f32[256,128]{1,0:T(8,128)S(1)} %maximum_select_fusion.1), channel_id=1, source_target_pairs={{0,0},{1,1},{2,10},{3,11},{4,20},{5,21},{6,30},{7,31},{8,2},{9,3},... | collective-permute-start | bytes 393224 | tf_op jit(solution)/shard_map/ppermute | solution.py:128
  99.7 5.3 %collective-permute-done.4.mirrored = f32[256,128]{1,0:T(8,128)S(1)} collective-permute-done((f32[256,128]{1,0:T(8,128)S(1)}, f32[256,128]{1,0:T(8,128)S(1)}, u32[]{:S(2)}, u32[]{:S(2)}) %collective-permute-start.4) | collective-permute-done | bytes 131104 | tf_op jit(solution)/shard_map/ppermute | solution.py:128
  105.0 3.4 %all-to-all-done.3.cube = f32[8,64,256]{2,1,0:T(8,128)S(1)} async-done(((f32[8,64,256]{2,1,0:T(8,128)}), f32[8,64,256]{2,1,0:T(8,128)S(1)}, u32[]{:S(2)}, u32[]{:S(2)}) %all-to-all-start.3) | async-done | bytes 524320 | tf_op jit(solution)/shard_map/all_to_all | solution.py:208
  108.4 0.8 shard_map.43
  (27 shorter events, 1.0 us)
Async XLA Ops:
  2.6 13.7 %copy-start.1 = (f32[128,256]{1,0:T(8,128)S(1)}, f32[128,256]{1,0:T(8,128)}, u32[]{:S(2)}) copy-start(f32[128,256]{1,0:T(8,128)} %param.2) | copy-start | bytes 393220
  2.6 35.4 %all-to-all-start = ((f32[8,128,256]{2,1,0:T(8,128)}), f32[8,128,256]{2,1,0:T(8,128)S(1)}, u32[]{:S(2)}, u32[]{:S(2)}) async-start(f32[8,128,256]{2,1,0:T(8,128)} %broadcast_in_dim.8), calls=%async_computation | async-start | bytes 2097152 | tf_op jit(solution)/shard_map/all_to_all | solution.py:165
  16.3 3.1 %collective-permute-start = (f32[64,256]{1,0:T(8,128)S(1)}, f32[64,256]{1,0:T(8,128)S(1)}, u32[]{:S(2)}, u32[]{:S(2)}) collective-permute-start(f32[64,256]{1,0:T(8,128)S(1)} %get-tuple-element.25), channel_id=1, source_target_pairs={{0,8},{8,0},{16,24},{24,16},{32,40},{40,32},{48,56},{56,48},{64,72... | collective-permute-start | bytes 196616 | tf_op jit(solution)/shard_map/ppermute | solution.py:109
  38.0 4.5 %collective-permute-start.1 = (f32[1024,256]{1,0:T(8,128)S(1)}, f32[1024,256]{1,0:T(8,128)S(1)}, u32[]{:S(2)}, u32[]{:S(2)}) collective-permute-start(f32[1024,256]{1,0:T(8,128)S(1)} %bitcast.25), channel_id=1, source_target_pairs={{0,8},{8,0},{16,24},{24,16},{32,40},{40,32},{48,56},{56,48},{64,72... | collective-permute-start | bytes 3145736 | tf_op jit(solution)/shard_map/ppermute | solution.py:109
  40.2 0.7 copy-start.2
  63.8 18.6 %all-to-all-start.2 = ((f32[8,64,512]{2,1,0:T(8,128)}), f32[8,64,512]{2,1,0:T(8,128)S(1)}, u32[]{:S(2)}, u32[]{:S(2)}) async-start(f32[8,64,512]{2,1,0:T(8,128)} %broadcast_in_dim.21), calls=%async_computation.2 | async-start | bytes 2097152 | tf_op jit(solution)/shard_map/all_to_all | solution.py:114
  70.0 3.1 %collective-permute-start.2 = (f32[2,64,128]{2,1,0:T(8,128)S(1)}, f32[2,64,128]{2,1,0:T(8,128)S(1)}, u32[]{:S(2)}, u32[]{:S(2)}) collective-permute-start(f32[2,64,128]{2,1,0:T(8,128)S(1)} %pad_maximum_fusion.2), channel_id=1, source_target_pairs={{0,8},{8,0},{16,24},{24,16},{32,40},{40,32},{48,56},{56,48},{64,72... | collective-permute-start | bytes 196616 | tf_op jit(solution)/shard_map/ppermute | solution.py:109
  73.2 6.2 %collective-permute-start.3 = (f32[128,128]{1,0:T(8,128)S(1)}, f32[128,128]{1,0:T(8,128)S(1)}, u32[]{:S(2)}, u32[]{:S(2)}) collective-permute-start(f32[128,128]{1,0:T(8,128)S(1)} %get-tuple-element.15), channel_id=1, source_target_pairs={{0,1},{1,0},{2,3},{3,2},{4,5},{5,4},{6,7},{7,6},{8,9},{9,8},{10,11... | collective-permute-start | bytes 196616 | tf_op jit(solution)/shard_map/ppermute | solution.py:132
  83.4 0.8 copy-start
  84.2 24.3 %all-to-all-start.3 = ((f32[8,64,256]{2,1,0:T(8,128)}), f32[8,64,256]{2,1,0:T(8,128)S(1)}, u32[]{:S(2)}, u32[]{:S(2)}) async-start(f32[8,64,256]{2,1,0:T(8,128)} %bitcast.29), calls=%async_computation.3 | async-start | bytes 1048576 | tf_op jit(solution)/shard_map/all_to_all | solution.py:208
  89.8 15.2 %collective-permute-start.4 = (f32[256,128]{1,0:T(8,128)S(1)}, f32[256,128]{1,0:T(8,128)S(1)}, u32[]{:S(2)}, u32[]{:S(2)}) collective-permute-start(f32[256,128]{1,0:T(8,128)S(1)} %maximum_select_fusion.1), channel_id=1, source_target_pairs={{0,0},{1,1},{2,10},{3,11},{4,20},{5,21},{6,30},{7,31},{8,2},{9,3},... | collective-permute-start | bytes 393224 | tf_op jit(solution)/shard_map/ppermute | solution.py:128
